TPU v7x, 32 devices: a whole 2x2x4 slice. The times are simulated.
32 devices in a mesh: orbit: 2 (over y), lon: 4 (over z), lat: 4 (over x, core).
Axes of the slice: x: 2, y: 2, z: 4, core: 2. Of those that a mesh axis runs over, the one named last changes fastest.
Arguments:
- kernel: float32 [20, 131072], P(None, ('orbit', 'lon', 'lat')), may hold values from 0.2 to 1.2
- residual: float32 [131072], P(('orbit', 'lon', 'lat')), may hold values from -6 to 6
- owner_block: int32 [131072, 1], P(('orbit', 'lon', 'lat')), may hold values from 0 to 15; in each aligned block of 4096 rows (0 to 4095, 4096 to 8191, ...) at most 1024 rows name the same one
- column: int32 [131072], P(('orbit', 'lon', 'lat')), may hold values from 0 to 1023
- time_step: int32 [131072], P(('orbit', 'lon', 'lat')), may hold values from 0 to 7
- horizontal: float32 [4, 72, 32, 512], P(None, None, 'lon', 'lat'), may hold values from 0.04 to 0.22
- vertical: float32 [71, 32, 512], P(None, 'lon', 'lat'), may hold values from 0.02 to 0.24
Outputs:
- adjoint_state: float32 [72, 32, 512], P(None, 'lon', 'lat')
- flux_gradient: float32 [32, 512], P('lon', 'lat')
Inputs may be any that keep to these rules, and one draw needn't show every extreme that they name: `owner_block`: among the soundings of one device no block is named more than 1024 times, and in some device's soundings one block is named exactly 1024 times.
All inputs are finite; a program needn't handle non-finite values.
Results may differ from a plain program's by a relative error of at most 0.0001.
Values sent between devices are 32-bit elements; how exact they have to be, the bound alone decides.
A program may use at most 128 MiB of HBM per device.

v0:
```python
import functools

import jax
import jax.numpy as jnp
import numpy as np
from jax import lax
from jax.experimental import pallas as pl
from jax.experimental.pallas import tpu as pltpu
from jax.sharding import PartitionSpec as P

STEPS = 8
CLON = 8
CLAT = 128
CELLS = CLON * CLAT
ROWS = 24
CHUNK = 256
F32 = jnp.float32
BF16 = jnp.bfloat16
VMEM_LIMIT = 48 * 1024 * 1024
NT = (((1,), (1,)), ((), ()))


def level_weights(levels, kernel_levels):
    one = np.float32
    heights = np.arange(levels, dtype=np.float32)
    centre = np.clip((heights + one(0.5)) * one(kernel_levels) / one(levels) - one(0.5),
                     one(0), one(kernel_levels - 1))
    knots = np.arange(kernel_levels, dtype=np.float32)
    return np.maximum(one(0), one(1) - np.abs(centre[:, None] - knots[None, :]))


def split(values):
    high = values.astype(BF16)
    return high, (values - high.astype(F32)).astype(BF16)


def pack_kernel(owners, capacity, starts_ref, kernel_ref, residual_ref, owner_ref, segment_ref,
                out_ref, data_ref, place_ref, sorted_ref):
    levels, count = kernel_ref.shape
    chunks = count // CHUNK
    half = data_ref.shape[0] // 2
    high, low = split(kernel_ref[...] * residual_ref[...])
    segment = segment_ref[...]
    spare = jnp.zeros((half - levels - 1, count), F32)
    seg_high = (segment // CLAT * CLAT).astype(F32)
    seg_low = (segment % CLAT).astype(F32)
    data_ref[0:half] = jnp.concatenate(
        [high.astype(F32), seg_high, spare], axis=0).astype(BF16)
    data_ref[half:] = jnp.concatenate(
        [low.astype(F32), seg_low, spare], axis=0).astype(BF16)

    names = lax.broadcasted_iota(jnp.int32, (owners, CHUNK), 0)
    earlier = (lax.broadcasted_iota(jnp.int32, (CHUNK, CHUNK), 0)
               < lax.broadcasted_iota(jnp.int32, (CHUNK, CHUNK), 1)).astype(F32).astype(BF16)
    totals = jnp.zeros((owners, 1), F32)
    for c in range(chunks):
        own = (owner_ref[:, c * CHUNK:(c + 1) * CHUNK] == names).astype(F32)
        totals = totals + jnp.sum(own, axis=1, keepdims=True)
    before = (lax.broadcasted_iota(jnp.int32, (owners, owners), 1)
              < lax.broadcasted_iota(jnp.int32, (owners, owners), 0)).astype(F32)
    carry = jnp.dot(before, jnp.broadcast_to(totals, (owners, CHUNK)),
                    precision=lax.Precision.HIGHEST, preferred_element_type=F32)[:, 0:1]
    for c in range(chunks):
        own = (owner_ref[:, c * CHUNK:(c + 1) * CHUNK] == names).astype(F32)
        inside = jnp.dot(own.astype(BF16), earlier, preferred_element_type=F32)
        place_ref[:, c * CHUNK:(c + 1) * CHUNK] = jnp.sum(
            own * (inside + carry), axis=0, keepdims=True).astype(jnp.int32)
        carry = carry + jnp.sum(own, axis=1, keepdims=True)

    def arrange(block, _):
        base = block * CHUNK
        target = lax.broadcasted_iota(jnp.int32, (CHUNK, count), 0) + base
        chosen = (target == place_ref[...]).astype(F32).astype(BF16)
        got = lax.dot_general(data_ref[...], chosen, NT, preferred_element_type=F32)
        sorted_ref[:, pl.ds(pl.multiple_of(base, CHUNK), CHUNK)] = got[0:ROWS] + got[half:half + ROWS]
        return 0

    lax.fori_loop(0, chunks, arrange, 0)
    sorted_ref[:, count:] = jnp.zeros((ROWS, sorted_ref.shape[1] - count), F32)
    window = capacity + CLAT
    slot = lax.broadcasted_iota(jnp.int32, (ROWS, capacity), 1)
    row = lax.broadcasted_iota(jnp.int32, (ROWS, capacity), 0)

    def hand_out(name, _):
        start = starts_ref[name]
        length = starts_ref[name + 1] - start
        aligned = start // CLAT * CLAT
        run = sorted_ref[:, pl.ds(pl.multiple_of(aligned, CLAT), window)]
        run = pltpu.roll(run, lax.rem(window - (start - aligned), window), 1)[:, 0:capacity]
        out_ref[name] = jnp.where((row == levels) & (slot >= length), -1.0, run)[0:levels + 1]
        return 0

    lax.fori_loop(0, owners, hand_out, 0)


def pack(kernel, residual, owner_block, column, time_step, owners, capacity):
    levels, count = kernel.shape
    owner = owner_block.reshape(1, count)
    segment = (time_step * CELLS + column).reshape(1, count)
    labels = jnp.arange(owners + 1, dtype=jnp.int32)
    starts = jnp.sum((owner < labels[:, None]).astype(jnp.int32), axis=1)
    vmem = pl.BlockSpec(memory_space=pltpu.VMEM)
    return pl.pallas_call(
        functools.partial(pack_kernel, owners, capacity),
        out_shape=jax.ShapeDtypeStruct((owners, levels + 1, capacity), F32),
        in_specs=[pl.BlockSpec(memory_space=pltpu.SMEM)] + [vmem] * 4,
        out_specs=vmem,
        scratch_shapes=[
            pltpu.VMEM((64, count), BF16),
            pltpu.VMEM((1, count), jnp.int32),
            pltpu.VMEM((ROWS, count + capacity + CLAT), F32),
        ],
        compiler_params=pltpu.CompilerParams(vmem_limit_bytes=VMEM_LIMIT),
    )(starts, kernel, residual.reshape(1, count), owner, segment)


def bin_kernel(levels, lons, lats, slots_ref, out_ref, got_ref, total_ref, send_sem, recv_sem):
    owners, _, capacity = slots_ref.shape
    lon, lat = lax.axis_index("lon"), lax.axis_index("lat")
    mesh_id = pl.DeviceIdType.MESH
    half = STEPS * ROWS
    width = min(capacity, 2 * CHUNK)

    def peer(d):
        return lax.rem(lon + d // lats, lons), lax.rem(lat + lax.rem(d, lats), lats)

    def slot_copy(d):
        to_lon, to_lat = peer(d)
        return pltpu.make_async_remote_copy(
            src_ref=slots_ref.at[to_lon * lats + to_lat], dst_ref=got_ref.at[d],
            send_sem=send_sem.at[d], recv_sem=recv_sem.at[d],
            device_id={"lon": to_lon, "lat": to_lat}, device_id_type=mesh_id)

    barrier = pltpu.get_barrier_semaphore()

    def greet(d, _):
        to_lon, to_lat = peer(d)
        pl.semaphore_signal(barrier, inc=1, device_id={"lon": to_lon, "lat": to_lat},
                            device_id_type=mesh_id)
        return 0

    lax.fori_loop(1, owners, greet, 0)
    pl.semaphore_wait(barrier, owners - 1)

    def turn(i):
        return jnp.where(lax.rem(i, 2) == 1, (i + 1) // 2, lax.rem(owners - i // 2, owners))

    def begin(i, _):
        slot_copy(turn(i)).start()
        return 0

    lax.fori_loop(1, owners, begin, 0)
    total_ref[...] = jnp.zeros_like(total_ref)
    got_ref[0] = slots_ref[lon * lats + lat]

    def collect(i, _):
        d = turn(i)

        @pl.when(i > 0)
        def _():
            slot_copy(d).wait_recv()

        for piece in range(capacity // width):
            rows = got_ref[d, :, piece * width:(piece + 1) * width]
            segment = rows[levels:levels + 1].astype(jnp.int32)
            values = jnp.concatenate(
                [rows[0:levels], jnp.zeros((ROWS - levels, width), F32)], axis=0)
            step = jnp.broadcast_to(segment >> 10, (ROWS, width))
            cell = segment & (CELLS - 1)
            place = lax.broadcasted_iota(jnp.int32, (CELLS, width), 0)
            chosen = (place == cell).astype(F32).astype(BF16)
            taken = jnp.concatenate(
                [jnp.where(step == j, values, 0.0) for j in range(STEPS)], axis=0)
            high = taken.astype(BF16)
            low = (taken - high.astype(F32)).astype(BF16)
            total_ref[...] += lax.dot_general(
                jnp.concatenate([high, low], axis=0), chosen, NT, preferred_element_type=F32)
        return 0

    lax.fori_loop(0, owners, collect, 0)
    for i in range(CLON):
        part = (total_ref[0:half, i * CLAT:(i + 1) * CLAT]
                + total_ref[half:, i * CLAT:(i + 1) * CLAT])
        for j in range(STEPS):
            out_ref[j, :, i, :] = part[j * ROWS:j * ROWS + levels]

    def finish(d, _):
        slot_copy(d).wait_send()
        return 0

    lax.fori_loop(1, owners, finish, 0)


def bin_soundings(slots, levels):
    lons, lats = lax.axis_size("lon"), lax.axis_size("lat")
    vmem = pl.BlockSpec(memory_space=pltpu.VMEM)
    return pl.pallas_call(
        functools.partial(bin_kernel, levels, lons, lats),
        out_shape=jax.ShapeDtypeStruct((STEPS, levels, CLON, CLAT), F32),
        in_specs=[vmem],
        out_specs=vmem,
        scratch_shapes=[
            pltpu.VMEM(slots.shape, F32),
            pltpu.VMEM((2 * STEPS * ROWS, CELLS), F32),
            pltpu.SemaphoreType.DMA((lons * lats,)),
            pltpu.SemaphoreType.DMA((lons * lats,)),
        ],
        compiler_params=pltpu.CompilerParams(
            collective_id=1, has_side_effects=True, vmem_limit_bytes=VMEM_LIMIT),
    )(slots)


def steps_kernel(orbits, lons, lats, weights, bins_ref, horizontal_ref, vertical_ref,
                 adjoint_ref, flux_ref, other_ref, forced_ref, mixed_ref, diagonal_ref, weight_ref,
                 edge_ref, lon_out, lon_in, lat_out, lat_in,
                 orbit_send, orbit_recv, edge_send, edge_recv):
    levels = adjoint_ref.shape[0]
    lon, lat, orbit = lax.axis_index("lon"), lax.axis_index("lat"), lax.axis_index("orbit")
    east, west = lax.rem(lon + 1, lons), lax.rem(lon + lons - 1, lons)
    partner = 1 - orbit
    mesh_id = pl.DeviceIdType.MESH
    barrier = pltpu.get_barrier_semaphore()
    pl.semaphore_signal(barrier, inc=1, device_id={"lon": east}, device_id_type=mesh_id)
    pl.semaphore_signal(barrier, inc=1, device_id={"lon": west}, device_id_type=mesh_id)
    pl.semaphore_signal(barrier, inc=1, device_id={"orbit": partner}, device_id_type=mesh_id)

    @pl.when(lat < lats - 1)
    def _():
        pl.semaphore_signal(barrier, inc=1, device_id={"lat": lat + 1}, device_id_type=mesh_id)

    @pl.when(lat > 0)
    def _():
        pl.semaphore_signal(barrier, inc=1, device_id={"lat": lat - 1}, device_id_type=mesh_id)

    peers = 3 + jnp.where(lat > 0, 1, 0) + jnp.where(lat < lats - 1, 1, 0)
    pl.semaphore_wait(barrier, peers)

    def orbit_copy(j):
        return pltpu.make_async_remote_copy(
            src_ref=bins_ref.at[j], dst_ref=other_ref.at[j],
            send_sem=orbit_send.at[j], recv_sem=orbit_recv.at[j],
            device_id={"orbit": partner}, device_id_type=mesh_id)

    def edge_copy(t, side):
        out, into = (lon_out, lon_in) if side < 2 else (lat_out, lat_in)
        device = ({"lon": east}, {"lon": west}, {"lat": lat + 1}, {"lat": lat - 1})[side]
        return pltpu.make_async_remote_copy(
            src_ref=out.at[side % 2, t], dst_ref=into.at[side % 2, t],
            send_sem=edge_send.at[side, t], recv_sem=edge_recv.at[side, t],
            device_id=device, device_id_type=mesh_id)

    def begin(t, _):
        orbit_copy(STEPS - 1 - t).start()
        return 0

    lax.fori_loop(0, STEPS, begin, 0)

    @pl.when(lat == 0)
    def _():
        lat_in[0] = jnp.zeros(lat_in.shape[1:], F32)

    @pl.when(lat == lats - 1)
    def _():
        lat_in[1] = jnp.zeros(lat_in.shape[1:], F32)

    part = (8, CLON, CLAT)
    lane = lax.broadcasted_iota(jnp.int32, part, 2)
    sub = lax.broadcasted_iota(jnp.int32, part, 1)
    level = lax.broadcasted_iota(jnp.int32, part, 0)
    chunks = range(0, levels, 8)
    pairs = CLAT // 2

    def gather_edge(total, values, side, first):
        column = values[:, :, CLAT - 1:CLAT] if side == 0 else values[:, :, 0:1]
        where = (2 * first - side) % CLAT
        place = (where + 2 * level) & (CLAT - 1)
        mine = jnp.sum(jnp.where(lane == place, jnp.broadcast_to(column, part), 0.0), axis=0)
        group = first // pairs
        total[group] = mine if total[group] is None else total[group] + mine

    groups = lat_in.shape[2]
    edge_weight = [[None] * groups, [None] * groups]
    for a in chunks:
        here = slice(a, a + 8)
        h = [horizontal_ref[d, here] for d in range(4)]
        diagonal_ref[here] = 1.0 - h[0] - h[1] - h[2] - h[3]
        weight_ref[0, here] = jnp.where(sub == 0, 0.0, pltpu.roll(h[0], 1, 1))
        weight_ref[1, here] = jnp.where(sub == CLON - 1, 0.0, pltpu.roll(h[1], CLON - 1, 1))
        weight_ref[2, here] = jnp.where(lane == 0, 0.0, pltpu.roll(h[2], 1, 2))
        weight_ref[3, here] = jnp.where(lane == CLAT - 1, 0.0, pltpu.roll(h[3], CLAT - 1, 2))
        gather_edge(edge_weight[0], h[2], 0, a)
        gather_edge(edge_weight[1], h[3], 1, a)
    for side in range(2):
        for g in range(groups):
            edge_ref[side, g] = edge_weight[side][g]

    def force(bins, a):
        forcing = []
        for l in range(a, a + 8):
            parts = [bins[k:k + 1] * float(weights[l, k]) for k in np.nonzero(weights[l])[0]]
            forcing.append(functools.reduce(lambda x, y: x + y, parts))
        return jnp.concatenate(forcing, axis=0)

    orbit_copy(STEPS - 1).wait_recv()
    bins = bins_ref[STEPS - 1] + other_ref[STEPS - 1]
    for a in chunks:
        forced_ref[a:a + 8] = force(bins, a)
    flux_ref[...] = jnp.zeros_like(flux_ref)
    none = jnp.zeros((1, CLON, CLAT), F32)

    def advance(t, _):
        edges = [[None] * groups, [None] * groups]
        for a in chunks:
            low, high = max(a - 1, 0), min(a + 9, levels)
            forced = forced_ref[low:high]
            up = vertical_ref[low:high - 1] * (forced[1:] - forced[:-1])
            if a == 0:
                up = jnp.concatenate([none, up], axis=0)
            if a + 8 == levels:
                up = jnp.concatenate([up, none], axis=0)
            mixed = forced_ref[a:a + 8] + up[1:] - up[:-1]
            mixed_ref[a:a + 8] = mixed
            gather_edge(edges[0], mixed, 0, a)
            gather_edge(edges[1], mixed, 1, a)
        lon_out[0, t] = horizontal_ref[0, :, CLON - 1, :] * mixed_ref[:, CLON - 1, :]
        edge_copy(t, 0).start()
        lon_out[1, t] = horizontal_ref[1, :, 0, :] * mixed_ref[:, 0, :]
        edge_copy(t, 1).start()
        for side in range(2):
            for g in range(groups):
                lat_out[side, t, g] = edge_ref[side, g] * edges[side][g]

        @pl.when(lat < lats - 1)
        def _():
            edge_copy(t, 2).start()

        @pl.when(lat > 0)
        def _():
            edge_copy(t, 3).start()

        for a in chunks:
            here = slice(a, a + 8)
            mixed = mixed_ref[here]
            adjoint_ref[here] = (diagonal_ref[here] * mixed
                                 + weight_ref[0, here] * pltpu.roll(mixed, 1, 1)
                                 + weight_ref[1, here] * pltpu.roll(mixed, CLON - 1, 1)
                                 + weight_ref[2, here] * pltpu.roll(mixed, 1, 2)
                                 + weight_ref[3, here] * pltpu.roll(mixed, CLAT - 1, 2))

        j = jnp.maximum(STEPS - 2 - t, 0)

        @pl.when(t < STEPS - 1)
        def _():
            orbit_copy(j).wait_recv()

        @pl.when(lat > 0)
        def _():
            edge_copy(t, 2).wait_recv()

        @pl.when(lat < lats - 1)
        def _():
            edge_copy(t, 3).wait_recv()

        edge_copy(t, 0).wait_recv()
        edge_copy(t, 1).wait_recv()
        adjoint_ref[:, 0, :] = adjoint_ref[:, 0, :] + lon_in[0, t]
        adjoint_ref[:, CLON - 1, :] = adjoint_ref[:, CLON - 1, :] + lon_in[1, t]
        bins = bins_ref[j] + other_ref[j]
        sides = [lat_in[0, t, g] + lat_in[1, t, g] for g in range(groups)]
        outer = (lane == 0) | (lane == CLAT - 1)
        for a in chunks:
            near = jnp.stack([pltpu.roll(sides[l // pairs], -2 * l % CLAT, 1)
                              for l in range(a, a + 8)])
            result = adjoint_ref[a:a + 8] + jnp.where(outer, near, 0.0)
            adjoint_ref[a:a + 8] = result
            forced_ref[a:a + 8] = result + force(bins, a)
            if a == 0:
                flux_ref[...] += result[0]
        return 0

    lax.fori_loop(0, STEPS, advance, 0)

    def finish(t, _):
        orbit_copy(t).wait_send()
        edge_copy(t, 0).wait_send()
        edge_copy(t, 1).wait_send()

        @pl.when(lat < lats - 1)
        def _():
            edge_copy(t, 2).wait_send()

        @pl.when(lat > 0)
        def _():
            edge_copy(t, 3).wait_send()

        return 0

    lax.fori_loop(0, STEPS, finish, 0)


def transport(bins, horizontal, vertical):
    levels = horizontal.shape[1]
    kernel_levels = bins.shape[1]
    orbits, lons, lats = (lax.axis_size(name) for name in ("orbit", "lon", "lat"))
    vmem = pl.BlockSpec(memory_space=pltpu.VMEM)
    block = (levels, CLON, CLAT)
    groups = -(-2 * levels // CLAT)
    return pl.pallas_call(
        functools.partial(steps_kernel, orbits, lons, lats, level_weights(levels, kernel_levels)),
        out_shape=(jax.ShapeDtypeStruct(block, F32), jax.ShapeDtypeStruct((CLON, CLAT), F32)),
        in_specs=[vmem] * 3,
        out_specs=(vmem, vmem),
        scratch_shapes=[
            pltpu.VMEM(bins.shape, F32),
            pltpu.VMEM(block, F32),
            pltpu.VMEM(block, F32),
            pltpu.VMEM(block, F32),
            pltpu.VMEM((4,) + block, F32),
            pltpu.VMEM((2, groups, CLON, CLAT), F32),
            pltpu.VMEM((2, STEPS, levels, CLAT), F32),
            pltpu.VMEM((2, STEPS, levels, CLAT), F32),
            pltpu.VMEM((2, STEPS, groups, CLON, CLAT), F32),
            pltpu.VMEM((2, STEPS, groups, CLON, CLAT), F32),
            pltpu.SemaphoreType.DMA((STEPS,)),
            pltpu.SemaphoreType.DMA((STEPS,)),
            pltpu.SemaphoreType.DMA((4, STEPS)),
            pltpu.SemaphoreType.DMA((4, STEPS)),
        ],
        compiler_params=pltpu.CompilerParams(
            collective_id=0, has_side_effects=True, vmem_limit_bytes=VMEM_LIMIT),
    )(bins, horizontal, vertical)


def per_device(kernel, residual, owner_block, column, time_step, horizontal, vertical):
    owners = lax.axis_size("lon") * lax.axis_size("lat")
    capacity = 4 * kernel.shape[1] // owners
    slots = pack(kernel, residual, owner_block, column, time_step, owners, capacity)
    return transport(bin_soundings(slots, kernel.shape[0]), horizontal, vertical)


def solution(mesh):
    placed = (
        P(None, ("orbit", "lon", "lat")),
        P(("orbit", "lon", "lat")),
        P(("orbit", "lon", "lat"), None),
        P(("orbit", "lon", "lat")),
        P(("orbit", "lon", "lat")),
        P(None, None, "lon", "lat"),
        P(None, "lon", "lat"),
    )
    return jax.shard_map(
        per_device,
        mesh=mesh,
        in_specs=placed,
        out_specs=(P(None, "lon", "lat"), P("lon", "lat")),
        check_vma=False,
    )
```

profile of v0, /device:TPU:0, one launch (start us, length us, event | category | flops | bytes accessed | tf_op | source)
XLA Modules:
  0.0 107.9 jit_solution(1424988912987898975)
XLA Ops:
  0.6 0.9 convert_reduce_fusion.starts_ref
  1.5 0.7 multiply_add_fusion
  2.2 0.0 copy-start.1
  2.2 1.0 copy-done.1
  3.2 0.0 copy-start.3
  3.2 0.7 copy-done.3
  4.0 0.0 copy-start.4
  4.0 0.7 copy-done.4
  4.7 15.2 %shard_map.86.slots_ref = f32[16,21,1024]{2,1,0:T(8,128)S(1)} custom-call(s32[17]{0:T(128)S(1)} %convert_reduce_fusion.starts_ref, f32[20,4096]{1,0:T(8,128)S(1)} %copy-done.1, f32[1,4096]{1,0:T(1,128)S(1)} %bitcast.7, s32[1,4096]{1,0:T(1,128)S(1)} %bitcast.6, s32[1,4096]{1,0:T(1,128)S(1)} %bitcast.4), custom_call_target="tpu_custom_call" | custom-call | tf_op jit(solution)/shard_map/pallas_call | solution.py:103
  19.9 0.0 copy-start
  19.9 0.0 copy-start.2
  19.9 43.4 %shard_map.87.bins_ref = f32[8,20,8,128]{3,2,1,0:T(8,128)S(1)} custom-call(f32[16,21,1024]{2,1,0:T(8,128)S(1)} %shard_map.86.slots_ref), custom_call_target="tpu_custom_call" | custom-call | tf_op jit(solution)/shard_map/pallas_call | solution.py:197
  63.3 0.0 copy-done
  63.4 0.0 copy-done.2
  63.4 43.2 %shard_map.88 = (f32[72,8,128]{2,1,0:T(8,128)S(1)}, f32[8,128]{1,0:T(8,128)S(1)}) custom-call(f32[8,20,8,128]{3,2,1,0:T(8,128)S(1)} %shard_map.87.bins_ref, f32[4,72,8,128]{3,2,1,0:T(8,128)S(1)} %copy-done, f32[71,8,128]{2,1,0:T(8,128)S(1)} %copy-done.2), custom_call_target="tpu_custom_call" | custom-call | tf_op jit(solution)/shard_map/pallas_call | solution.py:408
  106.6 0.7 copy.11
  107.3 0.6 copy.12
Async XLA Ops:
  2.2 1.0 copy-start.1
  3.2 0.7 copy-start.3
  4.0 0.7 copy-start.4
  19.9 43.4 %copy-start = (f32[4,72,8,128]{3,2,1,0:T(8,128)S(1)}, f32[4,72,8,128]{3,2,1,0:T(8,128)}, u32[]{:S(2)}) copy-start(f32[4,72,8,128]{3,2,1,0:T(8,128)} %horizontal_ref.1) | copy-start | bytes 3538948
  19.9 43.4 %copy-start.2 = (f32[71,8,128]{2,1,0:T(8,128)S(1)}, f32[71,8,128]{2,1,0:T(8,128)}, u32[]{:S(2)}) copy-start(f32[71,8,128]{2,1,0:T(8,128)} %vertical_ref.1) | copy-start | bytes 872452
where the time goes:
time: 109 us; the launch traced here: 108 us
  Pallas kernels  102 us (94%)
  local copies, waits for them, and re-layouts  3.75 us (3%)
  other arithmetic  1.62 us (1%)
    pallas_call x1, Pallas kernels, bin_soundings(): pl.pallas_call(functools.partial(bin_kernel, levels, lons, lats), out_sha...  43.4 us
    pallas_call x1, Pallas kernels, transport(): pl.pallas_call(functools.partial(steps_kernel, orbits, lons, lats, level_...  43.2 us
    pallas_call x1, Pallas kernels, pack(): pl.pallas_call(functools.partial(pack_kernel, owners, capacity), out_shap...  15.2 us
    unnamed x12, local copies, waits for them, and re-layouts  3.75 us

commit v1 on v0

--- a/solution.py
+++ b/solution.py
@@ -34,92 +34,123 @@
     return high, (values - high.astype(F32)).astype(BF16)
 
 
-def pack_kernel(owners, capacity, starts_ref, kernel_ref, residual_ref, owner_ref, segment_ref,
-                out_ref, data_ref, place_ref, sorted_ref):
-    levels, count = kernel_ref.shape
+def pack_kernel(owners, kernel_hbm, residual_hbm, owner_hbm, column_hbm, time_hbm, out_ref,
+                kernel_ref, residual_ref, owner_ref, column_ref, time_ref, own_ref, data_ref,
+                place_ref, left_ref, sorted_ref, sem):
+    levels, count = kernel_hbm.shape
+    slot_rows = out_ref.shape[2]
     chunks = count // CHUNK
-    half = data_ref.shape[0] // 2
-    high, low = split(kernel_ref[...] * residual_ref[...])
-    segment = segment_ref[...]
-    spare = jnp.zeros((half - levels - 1, count), F32)
-    seg_high = (segment // CLAT * CLAT).astype(F32)
-    seg_low = (segment % CLAT).astype(F32)
-    data_ref[0:half] = jnp.concatenate(
-        [high.astype(F32), seg_high, spare], axis=0).astype(BF16)
-    data_ref[half:] = jnp.concatenate(
-        [low.astype(F32), seg_low, spare], axis=0).astype(BF16)
-
-    names = lax.broadcasted_iota(jnp.int32, (owners, CHUNK), 0)
+    loads = [pltpu.make_async_copy(source, target, sem.at[i]) for i, (source, target) in enumerate(
+        ((owner_hbm, owner_ref), (column_hbm, column_ref), (time_hbm, time_ref),
+         (residual_hbm, residual_ref), (kernel_hbm, kernel_ref)))]
+    for load in loads:
+        load.start()
+    heights = sorted_ref.shape[1]
+    filled = count // CLAT
+    sorted_ref[:, filled:, :] = jnp.zeros((ROWS, heights - filled, CLAT), F32)
     earlier = (lax.broadcasted_iota(jnp.int32, (CHUNK, CHUNK), 0)
                < lax.broadcasted_iota(jnp.int32, (CHUNK, CHUNK), 1)).astype(F32).astype(BF16)
-    totals = jnp.zeros((owners, 1), F32)
-    for c in range(chunks):
-        own = (owner_ref[:, c * CHUNK:(c + 1) * CHUNK] == names).astype(F32)
-        totals = totals + jnp.sum(own, axis=1, keepdims=True)
+    names = lax.broadcasted_iota(jnp.int32, (owners, CHUNK), 0)
+    ones = jnp.ones((CHUNK, CLAT), F32).astype(BF16)
     before = (lax.broadcasted_iota(jnp.int32, (owners, owners), 1)
               < lax.broadcasted_iota(jnp.int32, (owners, owners), 0)).astype(F32)
-    carry = jnp.dot(before, jnp.broadcast_to(totals, (owners, CHUNK)),
-                    precision=lax.Precision.HIGHEST, preferred_element_type=F32)[:, 0:1]
+
+    loads[0].wait()
     for c in range(chunks):
-        own = (owner_ref[:, c * CHUNK:(c + 1) * CHUNK] == names).astype(F32)
-        inside = jnp.dot(own.astype(BF16), earlier, preferred_element_type=F32)
+        own_ref[c * owners:(c + 1) * owners] = (
+            owner_ref[:, c * CHUNK:(c + 1) * CHUNK] == names).astype(F32).astype(BF16)
+    inside = jnp.dot(own_ref[...], earlier, preferred_element_type=F32)
+    counts = jnp.dot(own_ref[...], ones, preferred_element_type=F32)
+    parts = [counts[c * owners:(c + 1) * owners] for c in range(chunks)]
+    totals = functools.reduce(lambda x, y: x + y, parts)
+    starts = jnp.dot(before, totals, precision=lax.Precision.HIGHEST, preferred_element_type=F32)
+    carry = starts
+    for c in range(chunks):
+        own = own_ref[c * owners:(c + 1) * owners].astype(F32)
+        wide = jnp.concatenate([carry] * (CHUNK // CLAT), axis=1)
         place_ref[:, c * CHUNK:(c + 1) * CHUNK] = jnp.sum(
-            own * (inside + carry), axis=0, keepdims=True).astype(jnp.int32)
-        carry = carry + jnp.sum(own, axis=1, keepdims=True)
-
-    def arrange(block, _):
-        base = block * CHUNK
-        target = lax.broadcasted_iota(jnp.int32, (CHUNK, count), 0) + base
-        chosen = (target == place_ref[...]).astype(F32).astype(BF16)
-        got = lax.dot_general(data_ref[...], chosen, NT, preferred_element_type=F32)
-        sorted_ref[:, pl.ds(pl.multiple_of(base, CHUNK), CHUNK)] = got[0:ROWS] + got[half:half + ROWS]
-        return 0
-
-    lax.fori_loop(0, chunks, arrange, 0)
-    sorted_ref[:, count:] = jnp.zeros((ROWS, sorted_ref.shape[1] - count), F32)
-    window = capacity + CLAT
-    slot = lax.broadcasted_iota(jnp.int32, (ROWS, capacity), 1)
-    row = lax.broadcasted_iota(jnp.int32, (ROWS, capacity), 0)
-
-    def hand_out(name, _):
-        start = starts_ref[name]
-        length = starts_ref[name + 1] - start
-        aligned = start // CLAT * CLAT
-        run = sorted_ref[:, pl.ds(pl.multiple_of(aligned, CLAT), window)]
-        run = pltpu.roll(run, lax.rem(window - (start - aligned), window), 1)[:, 0:capacity]
-        out_ref[name] = jnp.where((row == levels) & (slot >= length), -1.0, run)[0:levels + 1]
-        return 0
-
-    lax.fori_loop(0, owners, hand_out, 0)
+            own * (inside[c * owners:(c + 1) * owners] + wide), axis=0,
+            keepdims=True).astype(jnp.int32)
+        carry = carry + parts[c]
+
+    for load in loads[1:]:
+        load.wait()
+    high, low = split(kernel_ref[...] * residual_ref[...])
+    seg_high = (time_ref[...] * CLON + column_ref[...] // CLAT).astype(F32)
+    seg_low = (column_ref[...] % CLAT).astype(F32)
+    spare = jnp.zeros((ROWS - levels - 1, count), F32)
+    data_ref[...] = jnp.concatenate(
+        [high.astype(F32), seg_high * float(CLAT), spare, low.astype(F32), seg_low, spare],
+        axis=0).astype(BF16)
+
+    groups = count // CHUNK
+    span = min(count, 4 * CHUNK)
+    inner = lax.broadcasted_iota(jnp.int32, (CHUNK, span), 0).astype(F32).astype(BF16)
+    none = jnp.zeros((2 * ROWS, span), BF16)
+    total = None
+    for c in range(count // span):
+        here = slice(c * span, (c + 1) * span)
+        place = place_ref[:, here]
+        outer = jnp.broadcast_to((place // CHUNK).astype(F32), (2 * ROWS, span)).astype(BF16)
+        offset = jnp.broadcast_to((place % CHUNK).astype(F32), (CHUNK, span)).astype(BF16)
+        data = data_ref[:, here]
+        for g in range(groups):
+            left_ref[g * 2 * ROWS:(g + 1) * 2 * ROWS] = jnp.where(
+                outer == jnp.asarray(g, BF16), data, none)
+        chosen = jnp.where(offset == inner, jnp.ones((), BF16), jnp.zeros((), BF16))
+        got = lax.dot_general(left_ref[...], chosen, NT, preferred_element_type=F32)
+        total = got if total is None else total + got
+    for g in range(groups):
+        both = total[2 * ROWS * g:2 * ROWS * g + ROWS] + total[2 * ROWS * g + ROWS:2 * ROWS * (g + 1)]
+        for p in range(CHUNK // CLAT):
+            sorted_ref[:, g * (CHUNK // CLAT) + p, :] = both[:, p * CLAT:(p + 1) * CLAT]
+
+    shape = (levels + 1, slot_rows, CLAT)
+    lane = lax.broadcasted_iota(jnp.int32, shape, 2)
+    slot = (lax.broadcasted_iota(jnp.int32, (1, slot_rows, CLAT), 1) * CLAT
+            + lax.broadcasted_iota(jnp.int32, (1, slot_rows, CLAT), 2))
+    first = [jnp.max(starts[o:o + 1]).astype(jnp.int32) for o in range(owners)] + [count]
+    for o in range(owners):
+        row, shift = first[o] // CLAT, lax.rem(first[o], CLAT)
+        back = lax.rem(CLAT - shift, CLAT)
+        one = pltpu.roll(sorted_ref[0:levels + 1, pl.ds(row, slot_rows), :], back, 2)
+        two = pltpu.roll(sorted_ref[0:levels + 1, pl.ds(row + 1, slot_rows), :], back, 2)
+        run = jnp.where(lane < CLAT - shift, one, two)
+        out_ref[o, 0:levels] = run[0:levels]
+        out_ref[o, levels:] = jnp.where(slot < first[o + 1] - first[o], run[levels:], -1.0)
 
 
 def pack(kernel, residual, owner_block, column, time_step, owners, capacity):
     levels, count = kernel.shape
-    owner = owner_block.reshape(1, count)
-    segment = (time_step * CELLS + column).reshape(1, count)
-    labels = jnp.arange(owners + 1, dtype=jnp.int32)
-    starts = jnp.sum((owner < labels[:, None]).astype(jnp.int32), axis=1)
-    vmem = pl.BlockSpec(memory_space=pltpu.VMEM)
+    slot_rows = capacity // CLAT
+    heights = -(-(count // CLAT + slot_rows + 1) // 8) * 8
+    row = pltpu.VMEM((1, count), jnp.int32)
+    chunks = count // CHUNK
     return pl.pallas_call(
-        functools.partial(pack_kernel, owners, capacity),
-        out_shape=jax.ShapeDtypeStruct((owners, levels + 1, capacity), F32),
-        in_specs=[pl.BlockSpec(memory_space=pltpu.SMEM)] + [vmem] * 4,
-        out_specs=vmem,
+        functools.partial(pack_kernel, owners),
+        out_shape=jax.ShapeDtypeStruct((owners, levels + 1, slot_rows, CLAT), F32),
+        in_specs=[pl.BlockSpec(memory_space=pltpu.HBM)] * 5,
+        out_specs=pl.BlockSpec(memory_space=pltpu.VMEM),
         scratch_shapes=[
-            pltpu.VMEM((64, count), BF16),
-            pltpu.VMEM((1, count), jnp.int32),
-            pltpu.VMEM((ROWS, count + capacity + CLAT), F32),
+            pltpu.VMEM(kernel.shape, F32),
+            pltpu.VMEM((1, count), F32),
+            row, row, row,
+            pltpu.VMEM((chunks * owners, CHUNK), BF16),
+            pltpu.VMEM((2 * ROWS, count), BF16),
+            row,
+            pltpu.VMEM((2 * ROWS * chunks, min(count, 4 * CHUNK)), BF16),
+            pltpu.VMEM((ROWS, heights, CLAT), F32),
+            pltpu.SemaphoreType.DMA((5,)),
         ],
         compiler_params=pltpu.CompilerParams(vmem_limit_bytes=VMEM_LIMIT),
-    )(starts, kernel, residual.reshape(1, count), owner, segment)
-
-
-def bin_kernel(levels, lons, lats, slots_ref, out_ref, got_ref, total_ref, send_sem, recv_sem):
-    owners, _, capacity = slots_ref.shape
+    )(kernel, residual.reshape(1, count), owner_block.reshape(1, count),
+      column.reshape(1, count), time_step.reshape(1, count))
+
+
+def bin_kernel(levels, lons, lats, slots_ref, out_ref, got_ref, total_ref, left_ref, chosen_ref, send_sem, recv_sem):
+    owners, _, slot_rows, _ = slots_ref.shape
     lon, lat = lax.axis_index("lon"), lax.axis_index("lat")
     mesh_id = pl.DeviceIdType.MESH
-    half = STEPS * ROWS
-    width = min(capacity, 2 * CHUNK)
 
     def peer(d):
         return lax.rem(lon + d // lats, lons), lax.rem(lat + lax.rem(d, lats), lats)
@@ -160,29 +191,33 @@
         def _():
             slot_copy(d).wait_recv()
 
-        for piece in range(capacity // width):
-            rows = got_ref[d, :, piece * width:(piece + 1) * width]
-            segment = rows[levels:levels + 1].astype(jnp.int32)
-            values = jnp.concatenate(
-                [rows[0:levels], jnp.zeros((ROWS - levels, width), F32)], axis=0)
-            step = jnp.broadcast_to(segment >> 10, (ROWS, width))
-            cell = segment & (CELLS - 1)
-            place = lax.broadcasted_iota(jnp.int32, (CELLS, width), 0)
-            chosen = (place == cell).astype(F32).astype(BF16)
-            taken = jnp.concatenate(
-                [jnp.where(step == j, values, 0.0) for j in range(STEPS)], axis=0)
-            high = taken.astype(BF16)
-            low = (taken - high.astype(F32)).astype(BF16)
-            total_ref[...] += lax.dot_general(
-                jnp.concatenate([high, low], axis=0), chosen, NT, preferred_element_type=F32)
+        rows = jnp.concatenate([got_ref[d, :, i, :] for i in range(slot_rows)], axis=1)
+        width = rows.shape[1]
+        segment = rows[levels:levels + 1].astype(jnp.int32)
+        values = rows[0:levels]
+        high = values.astype(BF16).astype(F32)
+        spare = jnp.zeros((ROWS - levels, width), F32)
+        data = jnp.concatenate([high, spare, values - high, spare], axis=0).astype(BF16)
+        step = jnp.broadcast_to((segment >> 10).astype(F32), data.shape).astype(BF16)
+        for j in range(STEPS):
+            left_ref[j * 2 * ROWS:(j + 1) * 2 * ROWS] = jnp.where(
+                step == jnp.asarray(j, BF16), data, jnp.zeros(data.shape, BF16))
+        lane = lax.broadcasted_iota(jnp.int32, (CLAT, width), 0).astype(F32).astype(BF16)
+        for i in range(CLON):
+            key = jnp.where(((segment >> 7) & (CLON - 1)) == i, segment & (CLAT - 1), -1).astype(F32)
+            key = jnp.broadcast_to(key, (CLAT, width)).astype(BF16)
+            chosen_ref[i * CLAT:(i + 1) * CLAT] = jnp.where(
+                key == lane, jnp.ones((), BF16), jnp.zeros((), BF16))
+        total_ref[...] += lax.dot_general(
+            left_ref[...], chosen_ref[...], NT, preferred_element_type=F32)
         return 0
 
     lax.fori_loop(0, owners, collect, 0)
-    for i in range(CLON):
-        part = (total_ref[0:half, i * CLAT:(i + 1) * CLAT]
-                + total_ref[half:, i * CLAT:(i + 1) * CLAT])
-        for j in range(STEPS):
-            out_ref[j, :, i, :] = part[j * ROWS:j * ROWS + levels]
+    for j in range(STEPS):
+        top = j * 2 * ROWS
+        part = total_ref[top:top + levels] + total_ref[top + ROWS:top + ROWS + levels]
+        for i in range(CLON):
+            out_ref[j, :, i, :] = part[:, i * CLAT:(i + 1) * CLAT]
 
     def finish(d, _):
         slot_copy(d).wait_send()
@@ -202,6 +237,8 @@
         scratch_shapes=[
             pltpu.VMEM(slots.shape, F32),
             pltpu.VMEM((2 * STEPS * ROWS, CELLS), F32),
+            pltpu.VMEM((2 * STEPS * ROWS, slots.shape[2] * CLAT), BF16),
+            pltpu.VMEM((CELLS, slots.shape[2] * CLAT), BF16),
             pltpu.SemaphoreType.DMA((lons * lats,)),
             pltpu.SemaphoreType.DMA((lons * lats,)),
         ],

time: 109 us -> 92.3 us (0.85)
  Pallas kernels: 102 us -> 86 us
  other arithmetic: 1.62 us -> 0 us
  local copies, waits for them, and re-layouts: 3.75 us -> 5.18 us
    pallas_call x1, Pallas kernels: 15.2 us -> 3.49 us  [pack(): pl.pallas_call(functools.partial(pack_kernel, owners), out_shape=jax.Shap...]
    pallas_call x1, Pallas kernels: 43.4 us -> 39.2 us  [bin_soundings(): pl.pallas_call(functools.partial(bin_kernel, levels, lons, lats), out_sha...]
    unnamed x12 -> x16, local copies, waits for them, and re-layouts: 3.75 us -> 5.18 us
where the time goes in v1:
time: 92.3 us; the launch traced here: 91.8 us
  Pallas kernels  86 us (93%)
  local copies, waits for them, and re-layouts  5.18 us (6%)
    pallas_call x1, Pallas kernels, transport(): pl.pallas_call(functools.partial(steps_kernel, orbits, lons, lats, level_...  43.3 us
    pallas_call x1, Pallas kernels, bin_soundings(): pl.pallas_call(functools.partial(bin_kernel, levels, lons, lats), out_sha...  39.2 us
    unnamed x16, local copies, waits for them, and re-layouts  5.18 us
    pallas_call x1, Pallas kernels, pack(): pl.pallas_call(functools.partial(pack_kernel, owners), out_shape=jax.Shap...  3.49 us

profile of v1, /device:TPU:0, one launch (start us, length us, event | category | flops | bytes accessed | tf_op | source)
XLA Modules:
  0.0 91.8 jit_solution(3298518704552685085)
XLA Ops:
  0.6 0.0 copy-start.1
  0.6 1.0 %copy-done.1 = f32[20,4096]{1,0:T(8,128)S(1)} copy-done((f32[20,4096]{1,0:T(8,128)S(1)}, f32[20,4096]{1,0:T(8,128)}, u32[]{:S(2)}) %copy-start.1) | copy-done | bytes 327704
  1.6 0.0 copy-start.3
  1.6 0.7 copy-done.3
  2.3 0.0 copy-start.4
  2.3 0.7 copy-done.4
  3.1 0.0 copy-start.5
  3.1 0.7 copy-done.5
  3.8 0.0 copy-start.6
  3.8 0.7 copy-done.6
  4.5 3.5 %shard_map.86.slots_ref = f32[16,21,8,128]{3,2,1,0:T(8,128)S(1)} custom-call(f32[20,4096]{1,0:T(8,128)S(1)} %copy-done.1, f32[1,4096]{1,0:T(1,128)S(1)} %bitcast.4, s32[1,4096]{1,0:T(1,128)S(1)} %bitcast.5, s32[1,4096]{1,0:T(1,128)S(1)} %bitcast.6, s32[1,4096]{1,0:T(1,128)S(1)} %bitcast.7), custom_call_target="tpu_custom_call" | custom-call | tf_op jit(solution)/shard_map/pallas_call | solution.py:129
  8.0 0.0 copy-start
  8.0 0.0 copy-start.2
  8.0 39.2 %shard_map.87.bins_ref = f32[8,20,8,128]{3,2,1,0:T(8,128)S(1)} custom-call(f32[16,21,8,128]{3,2,1,0:T(8,128)S(1)} %shard_map.86.slots_ref), custom_call_target="tpu_custom_call" | custom-call | tf_op jit(solution)/shard_map/pallas_call | solution.py:232
  47.2 0.0 copy-done
  47.2 0.0 copy-done.2
  47.2 43.3 %shard_map.88 = (f32[72,8,128]{2,1,0:T(8,128)S(1)}, f32[8,128]{1,0:T(8,128)S(1)}) custom-call(f32[8,20,8,128]{3,2,1,0:T(8,128)S(1)} %shard_map.87.bins_ref, f32[4,72,8,128]{3,2,1,0:T(8,128)S(1)} %copy-done, f32[71,8,128]{2,1,0:T(8,128)S(1)} %copy-done.2), custom_call_target="tpu_custom_call" | custom-call | tf_op jit(solution)/shard_map/pallas_call | solution.py:445
  90.5 0.7 copy.11
  91.2 0.6 copy.12
Async XLA Ops:
  0.6 1.0 %copy-start.1 = (f32[20,4096]{1,0:T(8,128)S(1)}, f32[20,4096]{1,0:T(8,128)}, u32[]{:S(2)}) copy-start(f32[20,4096]{1,0:T(8,128)} %kernel_hbm.1) | copy-start | bytes 983044
  1.6 0.7 copy-start.3
  2.3 0.7 copy-start.4
  3.1 0.7 copy-start.5
  3.8 0.7 copy-start.6
  8.0 39.2 %copy-start = (f32[4,72,8,128]{3,2,1,0:T(8,128)S(1)}, f32[4,72,8,128]{3,2,1,0:T(8,128)}, u32[]{:S(2)}) copy-start(f32[4,72,8,128]{3,2,1,0:T(8,128)} %horizontal_ref.1) | copy-start | bytes 3538948
  8.0 39.2 %copy-start.2 = (f32[71,8,128]{2,1,0:T(8,128)S(1)}, f32[71,8,128]{2,1,0:T(8,128)}, u32[]{:S(2)}) copy-start(f32[71,8,128]{2,1,0:T(8,128)} %vertical_ref.1) | copy-start | bytes 872452

commit v2 on v1

--- a/solution.py
+++ b/solution.py
@@ -143,8 +143,9 @@
             pltpu.SemaphoreType.DMA((5,)),
         ],
         compiler_params=pltpu.CompilerParams(vmem_limit_bytes=VMEM_LIMIT),
-    )(kernel, residual.reshape(1, count), owner_block.reshape(1, count),
-      column.reshape(1, count), time_step.reshape(1, count))
+    )(*(pltpu.with_memory_space_constraint(x, pltpu.HBM) for x in (
+        kernel, residual.reshape(1, count), owner_block.reshape(1, count),
+        column.reshape(1, count), time_step.reshape(1, count))))
 
 
 def bin_kernel(levels, lons, lats, slots_ref, out_ref, got_ref, total_ref, left_ref, chosen_ref, send_sem, recv_sem):
@@ -249,28 +250,39 @@
 
 def steps_kernel(orbits, lons, lats, weights, bins_ref, horizontal_ref, vertical_ref,
                  adjoint_ref, flux_ref, other_ref, forced_ref, mixed_ref, diagonal_ref, weight_ref,
-                 edge_ref, lon_out, lon_in, lat_out, lat_in,
-                 orbit_send, orbit_recv, edge_send, edge_recv):
+                 first_ref, second_ref, halo_ref, pack_ref, lon_out, lon_in, lat_out, lat_in,
+                 diag_out, diag_in, orbit_send, orbit_recv, lon_send, lon_recv, lat_send, lat_recv,
+                 diag_send, diag_recv):
     levels = adjoint_ref.shape[0]
     lon, lat, orbit = lax.axis_index("lon"), lax.axis_index("lat"), lax.axis_index("orbit")
     east, west = lax.rem(lon + 1, lons), lax.rem(lon + lons - 1, lons)
     partner = 1 - orbit
     mesh_id = pl.DeviceIdType.MESH
+    pairs = STEPS // 2
+    last = CLON - 1
+    below, above = lat < lats - 1, lat > 0
     barrier = pltpu.get_barrier_semaphore()
-    pl.semaphore_signal(barrier, inc=1, device_id={"lon": east}, device_id_type=mesh_id)
-    pl.semaphore_signal(barrier, inc=1, device_id={"lon": west}, device_id_type=mesh_id)
-    pl.semaphore_signal(barrier, inc=1, device_id={"orbit": partner}, device_id_type=mesh_id)
-
-    @pl.when(lat < lats - 1)
+
+    def greet(device):
+        pl.semaphore_signal(barrier, inc=1, device_id=device, device_id_type=mesh_id)
+
+    greet({"lon": east})
+    greet({"lon": west})
+    greet({"orbit": partner})
+
+    @pl.when(below)
     def _():
-        pl.semaphore_signal(barrier, inc=1, device_id={"lat": lat + 1}, device_id_type=mesh_id)
-
-    @pl.when(lat > 0)
+        greet({"lat": lat + 1})
+        greet({"lon": east, "lat": lat + 1})
+        greet({"lon": west, "lat": lat + 1})
+
+    @pl.when(above)
     def _():
-        pl.semaphore_signal(barrier, inc=1, device_id={"lat": lat - 1}, device_id_type=mesh_id)
-
-    peers = 3 + jnp.where(lat > 0, 1, 0) + jnp.where(lat < lats - 1, 1, 0)
-    pl.semaphore_wait(barrier, peers)
+        greet({"lat": lat - 1})
+        greet({"lon": east, "lat": lat - 1})
+        greet({"lon": west, "lat": lat - 1})
+
+    pl.semaphore_wait(barrier, 3 + jnp.where(above, 3, 0) + jnp.where(below, 3, 0))
 
     def orbit_copy(j):
         return pltpu.make_async_remote_copy(
@@ -278,13 +290,27 @@
             send_sem=orbit_send.at[j], recv_sem=orbit_recv.at[j],
             device_id={"orbit": partner}, device_id_type=mesh_id)
 
-    def edge_copy(t, side):
-        out, into = (lon_out, lon_in) if side < 2 else (lat_out, lat_in)
-        device = ({"lon": east}, {"lon": west}, {"lat": lat + 1}, {"lat": lat - 1})[side]
+    def lon_copy(p, side):
         return pltpu.make_async_remote_copy(
-            src_ref=out.at[side % 2, t], dst_ref=into.at[side % 2, t],
-            send_sem=edge_send.at[side, t], recv_sem=edge_recv.at[side, t],
-            device_id=device, device_id_type=mesh_id)
+            src_ref=lon_out.at[side, p], dst_ref=lon_in.at[side, p],
+            send_sem=lon_send.at[side, p], recv_sem=lon_recv.at[side, p],
+            device_id={"lon": (east, west)[side]}, device_id_type=mesh_id)
+
+    def lat_copy(p, side):
+        return pltpu.make_async_remote_copy(
+            src_ref=lat_out.at[side, p], dst_ref=lat_in.at[side, p],
+            send_sem=lat_send.at[side, p], recv_sem=lat_recv.at[side, p],
+            device_id={"lat": (lat + 1, lat - 1)[side]}, device_id_type=mesh_id)
+
+    def diag_copy(p, side, turn):
+        return pltpu.make_async_remote_copy(
+            src_ref=diag_out.at[side, p], dst_ref=diag_in.at[side, turn, p],
+            send_sem=diag_send.at[side, turn, p], recv_sem=diag_recv.at[side, turn, p],
+            device_id={"lon": (east, west)[turn], "lat": (lat + 1, lat - 1)[side]},
+            device_id_type=mesh_id)
+
+    towards = (below, above)
+    comes = (above, below)
 
     def begin(t, _):
         orbit_copy(STEPS - 1 - t).start()
@@ -292,61 +318,72 @@
 
     lax.fori_loop(0, STEPS, begin, 0)
 
-    @pl.when(lat == 0)
-    def _():
-        lat_in[0] = jnp.zeros(lat_in.shape[1:], F32)
-
-    @pl.when(lat == lats - 1)
-    def _():
-        lat_in[1] = jnp.zeros(lat_in.shape[1:], F32)
+    for side in range(2):
+        @pl.when(jnp.logical_not(comes[side]))
+        def _():
+            lat_in[side] = jnp.zeros(lat_in.shape[1:], F32)
+            diag_in[side] = jnp.zeros(diag_in.shape[1:], F32)
 
     part = (8, CLON, CLAT)
     lane = lax.broadcasted_iota(jnp.int32, part, 2)
     sub = lax.broadcasted_iota(jnp.int32, part, 1)
     level = lax.broadcasted_iota(jnp.int32, part, 0)
     chunks = range(0, levels, 8)
-    pairs = CLAT // 2
-
-    def gather_edge(total, values, side, first):
-        column = values[:, :, CLAT - 1:CLAT] if side == 0 else values[:, :, 0:1]
-        where = (2 * first - side) % CLAT
-        place = (where + 2 * level) & (CLAT - 1)
-        mine = jnp.sum(jnp.where(lane == place, jnp.broadcast_to(column, part), 0.0), axis=0)
-        group = first // pairs
-        total[group] = mine if total[group] is None else total[group] + mine
-
-    groups = lat_in.shape[2]
-    edge_weight = [[None] * groups, [None] * groups]
+    ends = (CLAT - 1, 0)
+
+    def collect(total, values, side, first):
+        column = jnp.broadcast_to(values[:, :, ends[side]:ends[side] + 1], part)
+        mine = jnp.sum(jnp.where(lane == first + level, column, 0.0), axis=0)
+        return mine if total is None else total + mine
+
+    none = jnp.zeros((1, CLON, CLAT), F32)
+    packs = [[None] * 3, [None] * 3]
     for a in chunks:
         here = slice(a, a + 8)
         h = [horizontal_ref[d, here] for d in range(4)]
+        v = (jnp.concatenate([vertical_ref[a:levels - 1], none], axis=0) if a + 8 == levels
+             else vertical_ref[here])
+        mingled = jnp.where(sub == last, h[0], h[1])
+        for side in range(2):
+            for i, values in enumerate((v, h[2 + side], mingled)):
+                packs[side][i] = collect(packs[side][i], values, side, a)
         diagonal_ref[here] = 1.0 - h[0] - h[1] - h[2] - h[3]
         weight_ref[0, here] = jnp.where(sub == 0, 0.0, pltpu.roll(h[0], 1, 1))
-        weight_ref[1, here] = jnp.where(sub == CLON - 1, 0.0, pltpu.roll(h[1], CLON - 1, 1))
+        weight_ref[1, here] = jnp.where(sub == last, 0.0, pltpu.roll(h[1], last, 1))
         weight_ref[2, here] = jnp.where(lane == 0, 0.0, pltpu.roll(h[2], 1, 2))
         weight_ref[3, here] = jnp.where(lane == CLAT - 1, 0.0, pltpu.roll(h[3], CLAT - 1, 2))
-        gather_edge(edge_weight[0], h[2], 0, a)
-        gather_edge(edge_weight[1], h[3], 1, a)
     for side in range(2):
-        for g in range(groups):
-            edge_ref[side, g] = edge_weight[side][g]
-
-    def force(bins, a):
-        forcing = []
-        for l in range(a, a + 8):
-            parts = [bins[k:k + 1] * float(weights[l, k]) for k in np.nonzero(weights[l])[0]]
-            forcing.append(functools.reduce(lambda x, y: x + y, parts))
-        return jnp.concatenate(forcing, axis=0)
+        edge = (last, 0)[side]
+        lon_out[side, pairs, 0, 0:levels - 1] = vertical_ref[:, edge, :]
+        lon_out[side, pairs, 0, levels - 1:] = jnp.zeros((1, CLAT), F32)
+        lon_out[side, pairs, 1] = horizontal_ref[side, :, edge, :]
+        lat_out[side, pairs, 0] = packs[side][0]
+        lat_out[side, pairs, 1] = packs[side][1]
+        pack_ref[side, 0] = packs[side][1]
+        pack_ref[side, 1] = packs[side][2]
+        lon_copy(pairs, side).start()
+
+        @pl.when(towards[side])
+        def _():
+            lat_copy(pairs, side).start()
+
+    def force(j, target_ref):
+        bins = bins_ref[j] + other_ref[j]
+        for a in chunks:
+            forcing = []
+            for l in range(a, a + 8):
+                parts = [bins[k:k + 1] * float(weights[l, k]) for k in np.nonzero(weights[l])[0]]
+                forcing.append(functools.reduce(lambda x, y: x + y, parts))
+            target_ref[a:a + 8] = jnp.concatenate(forcing, axis=0)
 
     orbit_copy(STEPS - 1).wait_recv()
-    bins = bins_ref[STEPS - 1] + other_ref[STEPS - 1]
-    for a in chunks:
-        forced_ref[a:a + 8] = force(bins, a)
+    force(STEPS - 1, forced_ref)
+    orbit_copy(STEPS - 2).wait_recv()
+    force(STEPS - 2, second_ref)
     flux_ref[...] = jnp.zeros_like(flux_ref)
-    none = jnp.zeros((1, CLON, CLAT), F32)
-
-    def advance(t, _):
-        edges = [[None] * groups, [None] * groups]
+    halo_ref[...] = jnp.zeros_like(halo_ref)
+
+    def mix(packed):
         for a in chunks:
             low, high = max(a - 1, 0), min(a + 9, levels)
             forced = forced_ref[low:high]
@@ -357,82 +394,168 @@
                 up = jnp.concatenate([up, none], axis=0)
             mixed = forced_ref[a:a + 8] + up[1:] - up[:-1]
             mixed_ref[a:a + 8] = mixed
-            gather_edge(edges[0], mixed, 0, a)
-            gather_edge(edges[1], mixed, 1, a)
-        lon_out[0, t] = horizontal_ref[0, :, CLON - 1, :] * mixed_ref[:, CLON - 1, :]
-        edge_copy(t, 0).start()
-        lon_out[1, t] = horizontal_ref[1, :, 0, :] * mixed_ref[:, 0, :]
-        edge_copy(t, 1).start()
-        for side in range(2):
-            for g in range(groups):
-                lat_out[side, t, g] = edge_ref[side, g] * edges[side][g]
-
-        @pl.when(lat < lats - 1)
-        def _():
-            edge_copy(t, 2).start()
-
-        @pl.when(lat > 0)
-        def _():
-            edge_copy(t, 3).start()
-
+            if packed is not None:
+                for side in range(2):
+                    packed[side] = collect(packed[side], mixed, side, a)
+
+    def stencil(a):
+        here = slice(a, a + 8)
+        mixed = mixed_ref[here]
+        return (diagonal_ref[here] * mixed
+                + weight_ref[0, here] * pltpu.roll(mixed, 1, 1)
+                + weight_ref[1, here] * pltpu.roll(mixed, last, 1)
+                + weight_ref[2, here] * pltpu.roll(mixed, 1, 2)
+                + weight_ref[3, here] * pltpu.roll(mixed, CLAT - 1, 2))
+
+    def near(rows, a):
+        north = jnp.stack([pltpu.roll(rows[0], -l % CLAT, 1) for l in range(a, a + 8)])
+        south = jnp.stack([pltpu.roll(rows[1], CLAT - 1 - l, 1) for l in range(a, a + 8)])
+        return jnp.where(lane == 0, north, jnp.where(lane == CLAT - 1, south, 0.0))
+
+    wide = (levels, CLAT)
+    wide_lane = lax.broadcasted_iota(jnp.int32, wide, 1)
+    wide_level = lax.broadcasted_iota(jnp.int32, wide, 0)
+    flat_sub = lax.broadcasted_iota(jnp.int32, (CLON, CLAT), 0)
+    blank = jnp.zeros((1, CLAT), F32)
+
+    def upright(row):
+        return jnp.sum(jnp.where(wide_lane == wide_level, jnp.broadcast_to(row, wide), 0.0),
+                       axis=1, keepdims=True)
+
+    def advance(p, _):
+        packed = [None, None]
+        mix(packed)
+        shed = []
+        for side in range(2):
+            edge, inner = ((last, last - 1), (0, 1))[side]
+            mixed = mixed_ref[:, edge, :]
+            out = horizontal_ref[side, :, edge, :] * mixed
+            lon_out[side, p, 0] = out
+            lon_out[side, p, 1] = (
+                diagonal_ref[:, edge, :] * mixed
+                + weight_ref[side, :, edge, :] * mixed_ref[:, inner, :]
+                + weight_ref[2, :, edge, :] * pltpu.roll(mixed, 1, 1)
+                + weight_ref[3, :, edge, :] * pltpu.roll(mixed, CLAT - 1, 1)
+                + second_ref[:, edge, :])
+            lon_copy(p, side).start()
+        for side in range(2):
+            out = pack_ref[side, 0] * packed[side]
+            shed.append(out)
+            lat_out[side, p, 0] = out
+            diag_out[side, p, 0] = out
+            diag_out[side, p, 1] = pack_ref[side, 1] * packed[side]
+
+            @pl.when(towards[side])
+            def _():
+                diag_copy(p, side, 0).start()
+                diag_copy(p, side, 1).start()
+
+        partial = [None, None]
         for a in chunks:
             here = slice(a, a + 8)
-            mixed = mixed_ref[here]
-            adjoint_ref[here] = (diagonal_ref[here] * mixed
-                                 + weight_ref[0, here] * pltpu.roll(mixed, 1, 1)
-                                 + weight_ref[1, here] * pltpu.roll(mixed, CLON - 1, 1)
-                                 + weight_ref[2, here] * pltpu.roll(mixed, 1, 2)
-                                 + weight_ref[3, here] * pltpu.roll(mixed, CLAT - 1, 2))
-
-        j = jnp.maximum(STEPS - 2 - t, 0)
-
-        @pl.when(t < STEPS - 1)
+            local = stencil(a)
+            if a == 0:
+                flux_ref[...] += local[0]
+            local = local + second_ref[here]
+            forced_ref[here] = local
+            for side in range(2):
+                partial[side] = collect(partial[side], local, side, a)
+        for side in range(2):
+            lat_out[side, p, 1] = partial[side]
+
+            @pl.when(towards[side])
+            def _():
+                lat_copy(p, side).start()
+
+        @pl.when(p < pairs - 1)
         def _():
+            j = jnp.maximum(STEPS - 3 - 2 * p, 1)
             orbit_copy(j).wait_recv()
-
-        @pl.when(lat > 0)
+            force(j, first_ref)
+            orbit_copy(j - 1).wait_recv()
+            force(j - 1, second_ref)
+
+        @pl.when(p == 0)
         def _():
-            edge_copy(t, 2).wait_recv()
-
-        @pl.when(lat < lats - 1)
-        def _():
-            edge_copy(t, 3).wait_recv()
-
-        edge_copy(t, 0).wait_recv()
-        edge_copy(t, 1).wait_recv()
-        adjoint_ref[:, 0, :] = adjoint_ref[:, 0, :] + lon_in[0, t]
-        adjoint_ref[:, CLON - 1, :] = adjoint_ref[:, CLON - 1, :] + lon_in[1, t]
-        bins = bins_ref[j] + other_ref[j]
-        sides = [lat_in[0, t, g] + lat_in[1, t, g] for g in range(groups)]
-        outer = (lane == 0) | (lane == CLAT - 1)
+            for side in range(2):
+                lon_copy(pairs, side).wait_recv()
+
+                @pl.when(comes[side])
+                def _():
+                    lat_copy(pairs, side).wait_recv()
+
+        for side in range(2):
+            @pl.when(comes[side])
+            def _():
+                lat_copy(p, side).wait_recv()
+                diag_copy(p, side, 0).wait_recv()
+                diag_copy(p, side, 1).wait_recv()
+
+        for side in range(2):
+            lon_copy(p, side).wait_recv()
+            edge = (0, last)[side]
+            halo_ref[0, :, edge, :] = lon_in[side, p, 0]
+
+            far = (last, 0)[side]
+            corner = [upright(diag_in[i, side, p, 0, far:far + 1, :]) for i in range(2)]
+            beside = (lon_in[side, p, 1] + lon_out[1 - side, p, 0]
+                      + jnp.where(wide_lane == 0, corner[0], 0.0)
+                      + jnp.where(wide_lane == CLAT - 1, corner[1], 0.0))
+            up = lon_in[side, pairs, 0, 0:levels - 1] * (beside[1:] - beside[:-1])
+            mixed = (beside + jnp.concatenate([up, blank], axis=0)
+                     - jnp.concatenate([blank, up], axis=0))
+            halo_ref[1, :, edge, :] = lon_in[side, pairs, 1] * mixed
+
+        rows, later = [], []
+        for side in range(2):
+            rows.append(lat_in[side, p, 0])
+            beside = (lat_in[side, p, 1] + shed[1 - side]
+                      + jnp.where(flat_sub == 0, pltpu.roll(diag_in[side, 0, p, 1], 1, 0), 0.0)
+                      + jnp.where(flat_sub == last, pltpu.roll(diag_in[side, 1, p, 1], last, 0), 0.0))
+            up = lat_in[side, pairs, 0] * (pltpu.roll(beside, CLAT - 1, 1) - beside)
+            mixed = beside + up - pltpu.roll(up, 1, 1)
+            later.append(lat_in[side, pairs, 1] * mixed)
+
         for a in chunks:
-            near = jnp.stack([pltpu.roll(sides[l // pairs], -2 * l % CLAT, 1)
-                              for l in range(a, a + 8)])
-            result = adjoint_ref[a:a + 8] + jnp.where(outer, near, 0.0)
-            adjoint_ref[a:a + 8] = result
-            forced_ref[a:a + 8] = result + force(bins, a)
+            here = slice(a, a + 8)
+            more = halo_ref[0, here] + near(rows, a)
+            if a == 0:
+                flux_ref[...] += more[0]
+            forced_ref[here] += more
+        mix(None)
+        for a in chunks:
+            here = slice(a, a + 8)
+            result = stencil(a) + (halo_ref[1, here] + near(later, a))
             if a == 0:
                 flux_ref[...] += result[0]
-        return 0
-
-    lax.fori_loop(0, STEPS, advance, 0)
-
-    def finish(t, _):
+            adjoint_ref[here] = result
+            forced_ref[here] = result + first_ref[here]
+        return 0
+
+    first_ref[...] = jnp.zeros_like(first_ref)
+    lax.fori_loop(0, pairs, advance, 0)
+
+    def finish(p, _):
+        for side in range(2):
+            lon_copy(p, side).wait_send()
+
+            @pl.when(towards[side])
+            def _():
+                lat_copy(p, side).wait_send()
+
+            @pl.when(towards[side] & (p < pairs))
+            def _():
+                diag_copy(p, side, 0).wait_send()
+                diag_copy(p, side, 1).wait_send()
+        return 0
+
+    lax.fori_loop(0, pairs + 1, finish, 0)
+
+    def done(t, _):
         orbit_copy(t).wait_send()
-        edge_copy(t, 0).wait_send()
-        edge_copy(t, 1).wait_send()
-
-        @pl.when(lat < lats - 1)
-        def _():
-            edge_copy(t, 2).wait_send()
-
-        @pl.when(lat > 0)
-        def _():
-            edge_copy(t, 3).wait_send()
-
-        return 0
-
-    lax.fori_loop(0, STEPS, finish, 0)
+        return 0
+
+    lax.fori_loop(0, STEPS, done, 0)
 
 
 def transport(bins, horizontal, vertical):
@@ -441,7 +564,8 @@
     orbits, lons, lats = (lax.axis_size(name) for name in ("orbit", "lon", "lat"))
     vmem = pl.BlockSpec(memory_space=pltpu.VMEM)
     block = (levels, CLON, CLAT)
-    groups = -(-2 * levels // CLAT)
+    turns = STEPS // 2 + 1
+    flat = (CLON, CLAT)
     return pl.pallas_call(
         functools.partial(steps_kernel, orbits, lons, lats, level_weights(levels, kernel_levels)),
         out_shape=(jax.ShapeDtypeStruct(block, F32), jax.ShapeDtypeStruct((CLON, CLAT), F32)),
@@ -453,15 +577,24 @@
             pltpu.VMEM(block, F32),
             pltpu.VMEM(block, F32),
             pltpu.VMEM((4,) + block, F32),
-            pltpu.VMEM((2, groups, CLON, CLAT), F32),
-            pltpu.VMEM((2, STEPS, levels, CLAT), F32),
-            pltpu.VMEM((2, STEPS, levels, CLAT), F32),
-            pltpu.VMEM((2, STEPS, groups, CLON, CLAT), F32),
-            pltpu.VMEM((2, STEPS, groups, CLON, CLAT), F32),
+            pltpu.VMEM(block, F32),
+            pltpu.VMEM(block, F32),
+            pltpu.VMEM((2,) + block, F32),
+            pltpu.VMEM((2, 2) + flat, F32),
+            pltpu.VMEM((2, turns, 2, levels, CLAT), F32),
+            pltpu.VMEM((2, turns, 2, levels, CLAT), F32),
+            pltpu.VMEM((2, turns, 2) + flat, F32),
+            pltpu.VMEM((2, turns, 2) + flat, F32),
+            pltpu.VMEM((2, turns, 2) + flat, F32),
+            pltpu.VMEM((2, 2, turns, 2) + flat, F32),
             pltpu.SemaphoreType.DMA((STEPS,)),
             pltpu.SemaphoreType.DMA((STEPS,)),
-            pltpu.SemaphoreType.DMA((4, STEPS)),
-            pltpu.SemaphoreType.DMA((4, STEPS)),
+            pltpu.SemaphoreType.DMA((2, turns)),
+            pltpu.SemaphoreType.DMA((2, turns)),
+            pltpu.SemaphoreType.DMA((2, turns)),
+            pltpu.SemaphoreType.DMA((2, turns)),
+            pltpu.SemaphoreType.DMA((2, 2, turns)),
+            pltpu.SemaphoreType.DMA((2, 2, turns)),
         ],
         compiler_params=pltpu.CompilerParams(
             collective_id=0, has_side_effects=True, vmem_limit_bytes=VMEM_LIMIT),

time: 92.3 us -> 84 us (0.910)
  Pallas kernels: 86 us -> 81.7 us
  local copies, waits for them, and re-layouts: 5.18 us -> 1.32 us
    pallas_call x1, Pallas kernels: 43.3 us -> 38.6 us  [transport(): pl.pallas_call(functools.partial(steps_kernel, orbits, lons, lats, level_...]
    unnamed x16 -> x6, local copies, waits for them, and re-layouts: 5.18 us -> 1.32 us
where the time goes in v2:
time: 84 us; the launch traced here: 83.7 us
  Pallas kernels  81.7 us (97%)
  local copies, waits for them, and re-layouts  1.32 us (2%)
    pallas_call x1, Pallas kernels, bin_soundings(): pl.pallas_call(functools.partial(bin_kernel, levels, lons, lats), out_sha...  39.2 us
    pallas_call x1, Pallas kernels, transport(): pl.pallas_call(functools.partial(steps_kernel, orbits, lons, lats, level_...  38.6 us
    pallas_call x1, Pallas kernels, pack(): pl.pallas_call(functools.partial(pack_kernel, owners), out_shape=jax.Shap...  3.95 us

profile of v2, /device:TPU:0, one launch (start us, length us, event | category | flops | bytes accessed | tf_op | source)
XLA Modules:
  0.0 83.7 jit_solution(146387483511736042)
XLA Ops:
  0.6 4.0 %shard_map.86.slots_ref = f32[16,21,8,128]{3,2,1,0:T(8,128)S(1)} custom-call(f32[20,4096]{1,0:T(8,128)} %kernel_hbm.1, f32[1,4096]{1,0:T(1,128)} %bitcast.4, s32[1,4096]{1,0:T(1,128)} %bitcast.5, s32[1,4096]{1,0:T(1,128)} %bitcast.6, s32[1,4096]{1,0:T(1,128)} %bitcast.7), custom_call_target="tpu_custom_call" | custom-call | tf_op jit(solution)/shard_map/pallas_call | solution.py:129
  4.6 0.0 copy-start
  4.6 0.0 copy-start.1
  4.6 39.2 %shard_map.87.bins_ref = f32[8,20,8,128]{3,2,1,0:T(8,128)S(1)} custom-call(f32[16,21,8,128]{3,2,1,0:T(8,128)S(1)} %shard_map.86.slots_ref), custom_call_target="tpu_custom_call" | custom-call | tf_op jit(solution)/shard_map/pallas_call | solution.py:233
  43.8 0.0 copy-done
  43.8 0.0 copy-done.1
  43.9 38.6 %shard_map.88 = (f32[72,8,128]{2,1,0:T(8,128)S(1)}, f32[8,128]{1,0:T(8,128)S(1)}) custom-call(f32[8,20,8,128]{3,2,1,0:T(8,128)S(1)} %shard_map.87.bins_ref, f32[4,72,8,128]{3,2,1,0:T(8,128)S(1)} %copy-done, f32[71,8,128]{2,1,0:T(8,128)S(1)} %copy-done.1), custom_call_target="tpu_custom_call" | custom-call | tf_op jit(solution)/shard_map/pallas_call | solution.py:569
  82.4 0.7 copy.11
  83.1 0.6 copy.12
Async XLA Ops:
  4.6 39.3 %copy-start = (f32[4,72,8,128]{3,2,1,0:T(8,128)S(1)}, f32[4,72,8,128]{3,2,1,0:T(8,128)}, u32[]{:S(2)}) copy-start(f32[4,72,8,128]{3,2,1,0:T(8,128)} %horizontal_ref.1) | copy-start | bytes 3538948
  4.6 39.2 %copy-start.1 = (f32[71,8,128]{2,1,0:T(8,128)S(1)}, f32[71,8,128]{2,1,0:T(8,128)}, u32[]{:S(2)}) copy-start(f32[71,8,128]{2,1,0:T(8,128)} %vertical_ref.1) | copy-start | bytes 872452

commit v3 on v2

--- a/solution.py
+++ b/solution.py
@@ -174,8 +174,13 @@
     lax.fori_loop(1, owners, greet, 0)
     pl.semaphore_wait(barrier, owners - 1)
 
+    middle = lons // 2
+
     def turn(i):
-        return jnp.where(lax.rem(i, 2) == 1, (i + 1) // 2, lax.rem(owners - i // 2, owners))
+        ring = lax.rem(i + lons * lats - 1, owners) // lats
+        offset = middle + (ring + 1) // 2 * jnp.where(lax.rem(ring, 2) == 1, -1, 1)
+        other = offset * lats + lax.rem(i + lats - 1, lats)
+        return jnp.where(i == 0, 0, jnp.where(i <= owners - lats, other, i - owners + lats))
 
     def begin(i, _):
         slot_copy(turn(i)).start()
@@ -329,38 +334,49 @@
     sub = lax.broadcasted_iota(jnp.int32, part, 1)
     level = lax.broadcasted_iota(jnp.int32, part, 0)
     chunks = range(0, levels, 8)
-    ends = (CLAT - 1, 0)
-
-    def collect(total, values, side, first):
-        column = jnp.broadcast_to(values[:, :, ends[side]:ends[side] + 1], part)
-        mine = jnp.sum(jnp.where(lane == first + level, column, 0.0), axis=0)
-        return mine if total is None else total + mine
+    flat = (CLON, CLAT)
+    flat_lane = lax.broadcasted_iota(jnp.int32, flat, 1)
+    flat_sub = lax.broadcasted_iota(jnp.int32, flat, 0)
+    even = (flat_lane & 1) == 0
+
+    def collect(total, values, first):
+        for i in range(8):
+            l = first + i
+            pair = (flat_lane >= l) & (flat_lane <= l + 1)
+            total[l % 2] = jnp.where(pair, pltpu.roll(values[i], l + 1, 1), total[l % 2])
+
+    def gather():
+        return [jnp.zeros(flat, F32), jnp.zeros(flat, F32)]
+
+    def rows_of(total):
+        return (jnp.where(even, total[0], total[1]),
+                pltpu.roll(jnp.where(even, total[1], total[0]), CLAT - 1, 1))
 
     none = jnp.zeros((1, CLON, CLAT), F32)
-    packs = [[None] * 3, [None] * 3]
+    packs = [gather(), gather(), gather()]
     for a in chunks:
         here = slice(a, a + 8)
         h = [horizontal_ref[d, here] for d in range(4)]
         v = (jnp.concatenate([vertical_ref[a:levels - 1], none], axis=0) if a + 8 == levels
              else vertical_ref[here])
         mingled = jnp.where(sub == last, h[0], h[1])
-        for side in range(2):
-            for i, values in enumerate((v, h[2 + side], mingled)):
-                packs[side][i] = collect(packs[side][i], values, side, a)
+        for i, values in enumerate((v, jnp.where(lane == 0, h[3], h[2]), mingled)):
+            collect(packs[i], values, a)
         diagonal_ref[here] = 1.0 - h[0] - h[1] - h[2] - h[3]
         weight_ref[0, here] = jnp.where(sub == 0, 0.0, pltpu.roll(h[0], 1, 1))
         weight_ref[1, here] = jnp.where(sub == last, 0.0, pltpu.roll(h[1], last, 1))
         weight_ref[2, here] = jnp.where(lane == 0, 0.0, pltpu.roll(h[2], 1, 2))
         weight_ref[3, here] = jnp.where(lane == CLAT - 1, 0.0, pltpu.roll(h[3], CLAT - 1, 2))
+    packs = [rows_of(total) for total in packs]
     for side in range(2):
         edge = (last, 0)[side]
         lon_out[side, pairs, 0, 0:levels - 1] = vertical_ref[:, edge, :]
         lon_out[side, pairs, 0, levels - 1:] = jnp.zeros((1, CLAT), F32)
         lon_out[side, pairs, 1] = horizontal_ref[side, :, edge, :]
-        lat_out[side, pairs, 0] = packs[side][0]
-        lat_out[side, pairs, 1] = packs[side][1]
-        pack_ref[side, 0] = packs[side][1]
-        pack_ref[side, 1] = packs[side][2]
+        lat_out[side, pairs, 0] = packs[0][side]
+        lat_out[side, pairs, 1] = packs[1][side]
+        pack_ref[side, 0] = packs[1][side]
+        pack_ref[side, 1] = packs[2][side]
         lon_copy(pairs, side).start()
 
         @pl.when(towards[side])
@@ -395,8 +411,7 @@
             mixed = forced_ref[a:a + 8] + up[1:] - up[:-1]
             mixed_ref[a:a + 8] = mixed
             if packed is not None:
-                for side in range(2):
-                    packed[side] = collect(packed[side], mixed, side, a)
+                collect(packed, mixed, a)
 
     def stencil(a):
         here = slice(a, a + 8)
@@ -407,15 +422,19 @@
                 + weight_ref[2, here] * pltpu.roll(mixed, 1, 2)
                 + weight_ref[3, here] * pltpu.roll(mixed, CLAT - 1, 2))
 
-    def near(rows, a):
-        north = jnp.stack([pltpu.roll(rows[0], -l % CLAT, 1) for l in range(a, a + 8)])
-        south = jnp.stack([pltpu.roll(rows[1], CLAT - 1 - l, 1) for l in range(a, a + 8)])
-        return jnp.where(lane == 0, north, jnp.where(lane == CLAT - 1, south, 0.0))
+    outer = (lane == 0) | (lane == CLAT - 1)
+
+    def weave(rows):
+        south = pltpu.roll(rows[1], CLAT - 1, 1)
+        return jnp.where(even, rows[0], south), jnp.where(even, south, rows[0])
+
+    def near(woven, a):
+        both = jnp.stack([pltpu.roll(woven[l % 2], -l % CLAT, 1) for l in range(a, a + 8)])
+        return jnp.where(outer, both, 0.0)
 
     wide = (levels, CLAT)
     wide_lane = lax.broadcasted_iota(jnp.int32, wide, 1)
     wide_level = lax.broadcasted_iota(jnp.int32, wide, 0)
-    flat_sub = lax.broadcasted_iota(jnp.int32, (CLON, CLAT), 0)
     blank = jnp.zeros((1, CLAT), F32)
 
     def upright(row):
@@ -423,34 +442,44 @@
                        axis=1, keepdims=True)
 
     def advance(p, _):
-        packed = [None, None]
+        packed = gather()
         mix(packed)
+        packed = rows_of(packed)
         shed = []
+        for side in range(2):
+            out = pack_ref[side, 0] * packed[side]
+            shed.append(out)
+            lat_out[side, p, 0] = out
+            diag_out[side, p, 0] = out
+            diag_out[side, p, 1] = pack_ref[side, 1] * packed[side]
+
+            @pl.when(towards[side])
+            def _():
+                diag_copy(p, side, 0).start()
+                diag_copy(p, side, 1).start()
+
         for side in range(2):
             edge, inner = ((last, last - 1), (0, 1))[side]
             mixed = mixed_ref[:, edge, :]
-            out = horizontal_ref[side, :, edge, :] * mixed
-            lon_out[side, p, 0] = out
+            lon_out[side, p, 0] = horizontal_ref[side, :, edge, :] * mixed
             lon_out[side, p, 1] = (
                 diagonal_ref[:, edge, :] * mixed
                 + weight_ref[side, :, edge, :] * mixed_ref[:, inner, :]
                 + weight_ref[2, :, edge, :] * pltpu.roll(mixed, 1, 1)
                 + weight_ref[3, :, edge, :] * pltpu.roll(mixed, CLAT - 1, 1)
                 + second_ref[:, edge, :])
-            lon_copy(p, side).start()
-        for side in range(2):
-            out = pack_ref[side, 0] * packed[side]
-            shed.append(out)
-            lat_out[side, p, 0] = out
-            diag_out[side, p, 0] = out
-            diag_out[side, p, 1] = pack_ref[side, 1] * packed[side]
-
-            @pl.when(towards[side])
-            def _():
-                diag_copy(p, side, 0).start()
-                diag_copy(p, side, 1).start()
-
-        partial = [None, None]
+
+        @pl.when(lon == 0)
+        def _():
+            lon_copy(p, 1).start()
+            lon_copy(p, 0).start()
+
+        @pl.when(lon > 0)
+        def _():
+            lon_copy(p, 0).start()
+            lon_copy(p, 1).start()
+
+        partial = gather()
         for a in chunks:
             here = slice(a, a + 8)
             local = stencil(a)
@@ -458,8 +487,8 @@
                 flux_ref[...] += local[0]
             local = local + second_ref[here]
             forced_ref[here] = local
-            for side in range(2):
-                partial[side] = collect(partial[side], local, side, a)
+            collect(partial, local, a)
+        partial = rows_of(partial)
         for side in range(2):
             lat_out[side, p, 1] = partial[side]
 
@@ -516,6 +545,7 @@
             mixed = beside + up - pltpu.roll(up, 1, 1)
             later.append(lat_in[side, pairs, 1] * mixed)
 
+        rows, later = weave(rows), weave(later)
         for a in chunks:
             here = slice(a, a + 8)
             more = halo_ref[0, here] + near(rows, a)

time: 84 us -> 86.8 us (1.033)
  Pallas kernels: 81.7 us -> 84.5 us
    pallas_call x1, Pallas kernels: 39.2 us -> 43.3 us  [bin_soundings(): pl.pallas_call(functools.partial(bin_kernel, levels, lons, lats), out_sha...]
    pallas_call x1, Pallas kernels: 38.6 us -> 37.3 us  [transport(): pl.pallas_call(functools.partial(steps_kernel, orbits, lons, lats, level_...]
where the time goes in v3:
time: 86.8 us; the launch traced here: 86.5 us
  Pallas kernels  84.5 us (97%)
  local copies, waits for them, and re-layouts  1.32 us (2%)
    pallas_call x1, Pallas kernels, bin_soundings(): pl.pallas_call(functools.partial(bin_kernel, levels, lons, lats), out_sha...  43.3 us
    pallas_call x1, Pallas kernels, transport(): pl.pallas_call(functools.partial(steps_kernel, orbits, lons, lats, level_...  37.3 us
    pallas_call x1, Pallas kernels, pack(): pl.pallas_call(functools.partial(pack_kernel, owners), out_shape=jax.Shap...  3.95 us

profile of v3, /device:TPU:0, one launch (start us, length us, event | category | flops | bytes accessed | tf_op | source)
XLA Modules:
  0.0 86.5 jit_solution(12566066549240729076)
XLA Ops:
  0.6 4.0 %shard_map.86.slots_ref = f32[16,21,8,128]{3,2,1,0:T(8,128)S(1)} custom-call(f32[20,4096]{1,0:T(8,128)} %kernel_hbm.1, f32[1,4096]{1,0:T(1,128)} %bitcast.4, s32[1,4096]{1,0:T(1,128)} %bitcast.5, s32[1,4096]{1,0:T(1,128)} %bitcast.6, s32[1,4096]{1,0:T(1,128)} %bitcast.7), custom_call_target="tpu_custom_call" | custom-call | tf_op jit(solution)/shard_map/pallas_call | solution.py:129
  4.6 0.0 copy-start
  4.6 0.0 copy-start.1
  4.6 43.3 %shard_map.87.bins_ref = f32[8,20,8,128]{3,2,1,0:T(8,128)S(1)} custom-call(f32[16,21,8,128]{3,2,1,0:T(8,128)S(1)} %shard_map.86.slots_ref), custom_call_target="tpu_custom_call" | custom-call | tf_op jit(solution)/shard_map/pallas_call | solution.py:238
  47.9 0.0 copy-done
  47.9 0.0 copy-done.1
  47.9 37.3 %shard_map.88 = (f32[72,8,128]{2,1,0:T(8,128)S(1)}, f32[8,128]{1,0:T(8,128)S(1)}) custom-call(f32[8,20,8,128]{3,2,1,0:T(8,128)S(1)} %shard_map.87.bins_ref, f32[4,72,8,128]{3,2,1,0:T(8,128)S(1)} %copy-done, f32[71,8,128]{2,1,0:T(8,128)S(1)} %copy-done.1), custom_call_target="tpu_custom_call" | custom-call | tf_op jit(solution)/shard_map/pallas_call | solution.py:599
  85.2 0.7 copy.11
  85.9 0.6 copy.12
Async XLA Ops:
  4.6 43.3 %copy-start = (f32[4,72,8,128]{3,2,1,0:T(8,128)S(1)}, f32[4,72,8,128]{3,2,1,0:T(8,128)}, u32[]{:S(2)}) copy-start(f32[4,72,8,128]{3,2,1,0:T(8,128)} %horizontal_ref.1) | copy-start | bytes 3538948
  4.6 43.3 %copy-start.1 = (f32[71,8,128]{2,1,0:T(8,128)S(1)}, f32[71,8,128]{2,1,0:T(8,128)}, u32[]{:S(2)}) copy-start(f32[71,8,128]{2,1,0:T(8,128)} %vertical_ref.1) | copy-start | bytes 872452

commit v4 on v3

v4 whole, which is shorter than its diff:
```python
import functools

import jax
import jax.numpy as jnp
import numpy as np
from jax import lax
from jax.experimental import pallas as pl
from jax.experimental.pallas import tpu as pltpu
from jax.sharding import PartitionSpec as P

STEPS = 8
CLON = 8
CLAT = 128
CELLS = CLON * CLAT
ROWS = 24
CHUNK = 256
F32 = jnp.float32
BF16 = jnp.bfloat16
VMEM_LIMIT = 48 * 1024 * 1024
NT = (((1,), (1,)), ((), ()))


def level_weights(levels, kernel_levels):
    one = np.float32
    heights = np.arange(levels, dtype=np.float32)
    centre = np.clip((heights + one(0.5)) * one(kernel_levels) / one(levels) - one(0.5),
                     one(0), one(kernel_levels - 1))
    knots = np.arange(kernel_levels, dtype=np.float32)
    return np.maximum(one(0), one(1) - np.abs(centre[:, None] - knots[None, :]))


def split(values):
    high = values.astype(BF16)
    return high, (values - high.astype(F32)).astype(BF16)


def whole_kernel(orbits, lons, lats, weights, kernel_hbm, residual_hbm, owner_hbm, column_hbm, time_hbm,
                 horizontal_hbm, vertical_hbm, adjoint_ref, flux_ref,
                 kernel_ref, residual_ref, owner_ref, column_ref, time_ref, horizontal_ref, vertical_ref,
                 own_ref, data_ref, place_ref, left_ref, sorted_ref,
                 slots_ref, got_ref, total_ref, taken_ref, chosen_ref,
                 bins_ref, other_ref, forced_ref, mixed_ref, diagonal_ref, weight_ref,
                 first_ref, second_ref, halo_ref, pack_ref, lon_out, lon_in, lat_out, lat_in,
                 diag_out, diag_in, load_sem, slot_send, slot_recv, orbit_send, orbit_recv,
                 lon_send, lon_recv, lat_send, lat_recv, diag_send, diag_recv):
    klevels, count = kernel_hbm.shape
    owners, _, slot_rows, _ = slots_ref.shape
    chunks = count // CHUNK
    loads = [pltpu.make_async_copy(source, target, load_sem.at[i]) for i, (source, target) in enumerate(
        ((owner_hbm, owner_ref), (column_hbm, column_ref), (time_hbm, time_ref),
         (residual_hbm, residual_ref), (kernel_hbm, kernel_ref),
         (vertical_hbm, vertical_ref), (horizontal_hbm, horizontal_ref)))]
    for load in loads:
        load.start()
    heights = sorted_ref.shape[1]
    filled = count // CLAT
    sorted_ref[:, filled:, :] = jnp.zeros((ROWS, heights - filled, CLAT), F32)
    earlier = (lax.broadcasted_iota(jnp.int32, (CHUNK, CHUNK), 0)
               < lax.broadcasted_iota(jnp.int32, (CHUNK, CHUNK), 1)).astype(F32).astype(BF16)
    names = lax.broadcasted_iota(jnp.int32, (owners, CHUNK), 0)
    ones = jnp.ones((CHUNK, CLAT), F32).astype(BF16)
    before = (lax.broadcasted_iota(jnp.int32, (owners, owners), 1)
              < lax.broadcasted_iota(jnp.int32, (owners, owners), 0)).astype(F32)

    levels = adjoint_ref.shape[0]
    lon, lat, orbit = lax.axis_index("lon"), lax.axis_index("lat"), lax.axis_index("orbit")
    east, west = lax.rem(lon + 1, lons), lax.rem(lon + lons - 1, lons)
    partner = 1 - orbit
    mesh_id = pl.DeviceIdType.MESH
    pairs = STEPS // 2
    last = CLON - 1
    below, above = lat < lats - 1, lat > 0
    def peer(d):
        return lax.rem(lon + d // lats, lons), lax.rem(lat + lax.rem(d, lats), lats)

    def slot_copy(d):
        to_lon, to_lat = peer(d)
        return pltpu.make_async_remote_copy(
            src_ref=slots_ref.at[to_lon * lats + to_lat], dst_ref=got_ref.at[d],
            send_sem=slot_send.at[d], recv_sem=slot_recv.at[d],
            device_id={"lon": to_lon, "lat": to_lat}, device_id_type=mesh_id)

    barrier = pltpu.get_barrier_semaphore()
    pl.semaphore_signal(barrier, inc=1, device_id={"orbit": partner}, device_id_type=mesh_id)

    def greet(d, _):
        to_lon, to_lat = peer(d)
        pl.semaphore_signal(barrier, inc=1, device_id={"lon": to_lon, "lat": to_lat},
                            device_id_type=mesh_id)
        return 0

    lax.fori_loop(1, owners, greet, 0)

    def orbit_copy(j):
        return pltpu.make_async_remote_copy(
            src_ref=bins_ref.at[j], dst_ref=other_ref.at[j],
            send_sem=orbit_send.at[j], recv_sem=orbit_recv.at[j],
            device_id={"orbit": partner}, device_id_type=mesh_id)

    def lon_copy(p, side):
        return pltpu.make_async_remote_copy(
            src_ref=lon_out.at[side, p], dst_ref=lon_in.at[side, p],
            send_sem=lon_send.at[side, p], recv_sem=lon_recv.at[side, p],
            device_id={"lon": (east, west)[side]}, device_id_type=mesh_id)

    def lat_copy(p, side):
        return pltpu.make_async_remote_copy(
            src_ref=lat_out.at[side, p], dst_ref=lat_in.at[side, p],
            send_sem=lat_send.at[side, p], recv_sem=lat_recv.at[side, p],
            device_id={"lat": (lat + 1, lat - 1)[side]}, device_id_type=mesh_id)

    def diag_copy(p, side, turn):
        return pltpu.make_async_remote_copy(
            src_ref=diag_out.at[side, p], dst_ref=diag_in.at[side, turn, p],
            send_sem=diag_send.at[side, turn, p], recv_sem=diag_recv.at[side, turn, p],
            device_id={"lon": (east, west)[turn], "lat": (lat + 1, lat - 1)[side]},
            device_id_type=mesh_id)

    towards = (below, above)
    comes = (above, below)

    loads[0].wait()
    for c in range(chunks):
        own_ref[c * owners:(c + 1) * owners] = (
            owner_ref[:, c * CHUNK:(c + 1) * CHUNK] == names).astype(F32).astype(BF16)
    inside = jnp.dot(own_ref[...], earlier, preferred_element_type=F32)
    counts = jnp.dot(own_ref[...], ones, preferred_element_type=F32)
    parts = [counts[c * owners:(c + 1) * owners] for c in range(chunks)]
    totals = functools.reduce(lambda x, y: x + y, parts)
    starts = jnp.dot(before, totals, precision=lax.Precision.HIGHEST, preferred_element_type=F32)
    carry = starts
    for c in range(chunks):
        own = own_ref[c * owners:(c + 1) * owners].astype(F32)
        wide = jnp.concatenate([carry] * (CHUNK // CLAT), axis=1)
        place_ref[:, c * CHUNK:(c + 1) * CHUNK] = jnp.sum(
            own * (inside[c * owners:(c + 1) * owners] + wide), axis=0,
            keepdims=True).astype(jnp.int32)
        carry = carry + parts[c]


    pl.semaphore_wait(barrier, owners)
    loads[5].wait()
    loads[6].wait()
    for side in range(2):
        edge = (last, 0)[side]
        lon_out[side, pairs, 0, 0:levels - 1] = vertical_ref[:, edge, :]
        lon_out[side, pairs, 0, levels - 1:] = jnp.zeros((1, CLAT), F32)
        lon_out[side, pairs, 1] = horizontal_ref[side, :, edge, :]
        lon_copy(pairs, side).start()

    for load in loads[1:5]:
        load.wait()
    high, low = split(kernel_ref[...] * residual_ref[...])
    seg_high = (time_ref[...] * CLON + column_ref[...] // CLAT).astype(F32)
    seg_low = (column_ref[...] % CLAT).astype(F32)
    spare = jnp.zeros((ROWS - klevels - 1, count), F32)
    data_ref[...] = jnp.concatenate(
        [high.astype(F32), seg_high * float(CLAT), spare, low.astype(F32), seg_low, spare],
        axis=0).astype(BF16)

    groups = count // CHUNK
    span = min(count, 4 * CHUNK)
    inner = lax.broadcasted_iota(jnp.int32, (CHUNK, span), 0).astype(F32).astype(BF16)
    none = jnp.zeros((2 * ROWS, span), BF16)
    product = None
    for c in range(count // span):
        here = slice(c * span, (c + 1) * span)
        place = place_ref[:, here]
        outer = jnp.broadcast_to((place // CHUNK).astype(F32), (2 * ROWS, span)).astype(BF16)
        offset = jnp.broadcast_to((place % CHUNK).astype(F32), (CHUNK, span)).astype(BF16)
        data = data_ref[:, here]
        for g in range(groups):
            left_ref[g * 2 * ROWS:(g + 1) * 2 * ROWS] = jnp.where(
                outer == jnp.asarray(g, BF16), data, none)
        chosen = jnp.where(offset == inner, jnp.ones((), BF16), jnp.zeros((), BF16))
        got = lax.dot_general(left_ref[...], chosen, NT, preferred_element_type=F32)
        product = got if product is None else product + got
    for g in range(groups):
        both = product[2 * ROWS * g:2 * ROWS * g + ROWS] + product[2 * ROWS * g + ROWS:2 * ROWS * (g + 1)]
        for p in range(CHUNK // CLAT):
            sorted_ref[:, g * (CHUNK // CLAT) + p, :] = both[:, p * CLAT:(p + 1) * CLAT]

    shape = (klevels + 1, slot_rows, CLAT)
    slot_lane = lax.broadcasted_iota(jnp.int32, shape, 2)
    slot = (lax.broadcasted_iota(jnp.int32, (1, slot_rows, CLAT), 1) * CLAT
            + lax.broadcasted_iota(jnp.int32, (1, slot_rows, CLAT), 2))
    first = [jnp.clip(jnp.max(starts[o:o + 1]).astype(jnp.int32), 0, count)
             for o in range(owners)] + [count]
    for o in range(owners):
        row, shift = first[o] // CLAT, lax.rem(first[o], CLAT)
        back = lax.rem(CLAT - shift, CLAT)
        one = pltpu.roll(sorted_ref[0:klevels + 1, pl.ds(row, slot_rows), :], back, 2)
        two = pltpu.roll(sorted_ref[0:klevels + 1, pl.ds(row + 1, slot_rows), :], back, 2)
        run = jnp.where(slot_lane < CLAT - shift, one, two)
        slots_ref[o, 0:klevels] = run[0:klevels]
        slots_ref[o, klevels:] = jnp.where(slot < first[o + 1] - first[o], run[klevels:], -1.0)


    even_lon = lax.rem(lon, 2) == 0

    def send_turn(i):
        m = jnp.where(lax.rem(i, 2) == 1, i // 2, owners // 2 + i // 2 - 1)
        ring = m // lats
        right = (lax.rem(ring, 2) == 1) == even_lon
        offset = lons // 2 + (ring + 1) // 2 * jnp.where(right, 1, -1)
        return lax.rem(m, lats) + jnp.where(ring == lons - 1, 1, offset * lats)

    def turn(i):
        ring = i // lats
        offset = jnp.where(even_lon, lax.rem(lons - ring, lons), ring)
        return offset * lats + lax.rem(i, lats)

    def begin(i, _):
        slot_copy(send_turn(i)).start()
        return 0

    lax.fori_loop(1, owners, begin, 0)
    total_ref[...] = jnp.zeros_like(total_ref)
    got_ref[0] = slots_ref[lon * lats + lat]

    for side in range(2):
        @pl.when(jnp.logical_not(comes[side]))
        def _():
            lat_in[side] = jnp.zeros(lat_in.shape[1:], F32)
            diag_in[side] = jnp.zeros(diag_in.shape[1:], F32)

    part = (8, CLON, CLAT)
    lane = lax.broadcasted_iota(jnp.int32, part, 2)
    sub = lax.broadcasted_iota(jnp.int32, part, 1)
    level = lax.broadcasted_iota(jnp.int32, part, 0)
    tiles = range(0, levels, 8)
    flat = (CLON, CLAT)
    flat_lane = lax.broadcasted_iota(jnp.int32, flat, 1)
    flat_sub = lax.broadcasted_iota(jnp.int32, flat, 0)
    even = (flat_lane & 1) == 0

    def collect(total, values, first):
        for i in range(8):
            l = first + i
            pair = (flat_lane >= l) & (flat_lane <= l + 1)
            total[l % 2] = jnp.where(pair, pltpu.roll(values[i], l + 1, 1), total[l % 2])

    def gather():
        return [jnp.zeros(flat, F32), jnp.zeros(flat, F32)]

    def rows_of(total):
        return (jnp.where(even, total[0], total[1]),
                pltpu.roll(jnp.where(even, total[1], total[0]), CLAT - 1, 1))

    none = jnp.zeros((1, CLON, CLAT), F32)
    packs = [gather(), gather(), gather()]
    for a in tiles:
        here = slice(a, a + 8)
        h = [horizontal_ref[d, here] for d in range(4)]
        v = (jnp.concatenate([vertical_ref[a:levels - 1], none], axis=0) if a + 8 == levels
             else vertical_ref[here])
        mingled = jnp.where(sub == last, h[0], h[1])
        for i, values in enumerate((v, jnp.where(lane == 0, h[3], h[2]), mingled)):
            collect(packs[i], values, a)
        diagonal_ref[here] = 1.0 - h[0] - h[1] - h[2] - h[3]
        weight_ref[0, here] = jnp.where(sub == 0, 0.0, pltpu.roll(h[0], 1, 1))
        weight_ref[1, here] = jnp.where(sub == last, 0.0, pltpu.roll(h[1], last, 1))
        weight_ref[2, here] = jnp.where(lane == 0, 0.0, pltpu.roll(h[2], 1, 2))
        weight_ref[3, here] = jnp.where(lane == CLAT - 1, 0.0, pltpu.roll(h[3], CLAT - 1, 2))
    packs = [rows_of(total) for total in packs]
    for side in range(2):
        lat_out[side, pairs, 0] = packs[0][side]
        lat_out[side, pairs, 1] = packs[1][side]
        pack_ref[side, 0] = packs[1][side]
        pack_ref[side, 1] = packs[2][side]

        @pl.when(towards[side])
        def _():
            lat_copy(pairs, side).start()

    def gain(i, _):
        d = turn(i)

        @pl.when(i > 0)
        def _():
            slot_copy(d).wait_recv()

        rows = jnp.concatenate([got_ref[d, :, i, :] for i in range(slot_rows)], axis=1)
        width = rows.shape[1]
        segment = rows[klevels:klevels + 1].astype(jnp.int32)
        values = rows[0:klevels]
        high = values.astype(BF16).astype(F32)
        spare = jnp.zeros((ROWS - klevels, width), F32)
        data = jnp.concatenate([high, spare, values - high, spare], axis=0).astype(BF16)
        step = jnp.broadcast_to((segment >> 10).astype(F32), data.shape).astype(BF16)
        for j in range(STEPS):
            taken_ref[j * 2 * ROWS:(j + 1) * 2 * ROWS] = jnp.where(
                step == jnp.asarray(j, BF16), data, jnp.zeros(data.shape, BF16))
        cell = lax.broadcasted_iota(jnp.int32, (CLAT, width), 0).astype(F32).astype(BF16)
        for i in range(CLON):
            key = jnp.where(((segment >> 7) & (CLON - 1)) == i, segment & (CLAT - 1), -1).astype(F32)
            key = jnp.broadcast_to(key, (CLAT, width)).astype(BF16)
            chosen_ref[i * CLAT:(i + 1) * CLAT] = jnp.where(
                key == cell, jnp.ones((), BF16), jnp.zeros((), BF16))
        total_ref[...] += lax.dot_general(
            taken_ref[...], chosen_ref[...], NT, preferred_element_type=F32)
        return 0

    lax.fori_loop(0, owners, gain, 0)
    for j in range(STEPS - 1, -1, -1):
        top = j * 2 * ROWS
        cells = total_ref[top:top + klevels] + total_ref[top + ROWS:top + ROWS + klevels]
        for i in range(CLON):
            bins_ref[j, :, i, :] = cells[:, i * CLAT:(i + 1) * CLAT]
        orbit_copy(j).start()

    def force(j, target_ref):
        bins = bins_ref[j] + other_ref[j]
        for a in tiles:
            forcing = []
            for l in range(a, a + 8):
                parts = [bins[k:k + 1] * float(weights[l, k]) for k in np.nonzero(weights[l])[0]]
                forcing.append(functools.reduce(lambda x, y: x + y, parts))
            target_ref[a:a + 8] = jnp.concatenate(forcing, axis=0)

    orbit_copy(STEPS - 1).wait_recv()
    force(STEPS - 1, forced_ref)
    orbit_copy(STEPS - 2).wait_recv()
    force(STEPS - 2, second_ref)
    flux_ref[...] = jnp.zeros_like(flux_ref)
    halo_ref[...] = jnp.zeros_like(halo_ref)

    def mix(packed):
        for a in tiles:
            low, high = max(a - 1, 0), min(a + 9, levels)
            forced = forced_ref[low:high]
            up = vertical_ref[low:high - 1] * (forced[1:] - forced[:-1])
            if a == 0:
                up = jnp.concatenate([none, up], axis=0)
            if a + 8 == levels:
                up = jnp.concatenate([up, none], axis=0)
            mixed = forced_ref[a:a + 8] + up[1:] - up[:-1]
            mixed_ref[a:a + 8] = mixed
            if packed is not None:
                collect(packed, mixed, a)

    def stencil(a):
        here = slice(a, a + 8)
        mixed = mixed_ref[here]
        return (diagonal_ref[here] * mixed
                + weight_ref[0, here] * pltpu.roll(mixed, 1, 1)
                + weight_ref[1, here] * pltpu.roll(mixed, last, 1)
                + weight_ref[2, here] * pltpu.roll(mixed, 1, 2)
                + weight_ref[3, here] * pltpu.roll(mixed, CLAT - 1, 2))

    outer = (lane == 0) | (lane == CLAT - 1)

    def weave(rows):
        south = pltpu.roll(rows[1], CLAT - 1, 1)
        return jnp.where(even, rows[0], south), jnp.where(even, south, rows[0])

    def near(woven, a):
        both = jnp.stack([pltpu.roll(woven[l % 2], -l % CLAT, 1) for l in range(a, a + 8)])
        return jnp.where(outer, both, 0.0)

    wide = (levels, CLAT)
    wide_lane = lax.broadcasted_iota(jnp.int32, wide, 1)
    wide_level = lax.broadcasted_iota(jnp.int32, wide, 0)
    blank = jnp.zeros((1, CLAT), F32)

    def upright(row):
        return jnp.sum(jnp.where(wide_lane == wide_level, jnp.broadcast_to(row, wide), 0.0),
                       axis=1, keepdims=True)

    def advance(p, _):
        packed = gather()
        mix(packed)
        packed = rows_of(packed)
        shed = []
        for side in range(2):
            out = pack_ref[side, 0] * packed[side]
            shed.append(out)
            lat_out[side, p, 0] = out
            diag_out[side, p, 0] = out
            diag_out[side, p, 1] = pack_ref[side, 1] * packed[side]

            @pl.when(towards[side])
            def _():
                diag_copy(p, side, 0).start()
                diag_copy(p, side, 1).start()

        for side in range(2):
            edge, inner = ((last, last - 1), (0, 1))[side]
            mixed = mixed_ref[:, edge, :]
            lon_out[side, p, 0] = horizontal_ref[side, :, edge, :] * mixed
            lon_out[side, p, 1] = (
                diagonal_ref[:, edge, :] * mixed
                + weight_ref[side, :, edge, :] * mixed_ref[:, inner, :]
                + weight_ref[2, :, edge, :] * pltpu.roll(mixed, 1, 1)
                + weight_ref[3, :, edge, :] * pltpu.roll(mixed, CLAT - 1, 1)
                + second_ref[:, edge, :])

        @pl.when(lon == 0)
        def _():
            lon_copy(p, 1).start()
            lon_copy(p, 0).start()

        @pl.when(lon > 0)
        def _():
            lon_copy(p, 0).start()
            lon_copy(p, 1).start()

        partial = gather()
        for a in tiles:
            here = slice(a, a + 8)
            local = stencil(a)
            if a == 0:
                flux_ref[...] += local[0]
            local = local + second_ref[here]
            forced_ref[here] = local
            collect(partial, local, a)
        partial = rows_of(partial)
        for side in range(2):
            lat_out[side, p, 1] = partial[side]

            @pl.when(towards[side])
            def _():
                lat_copy(p, side).start()

        @pl.when(p < pairs - 1)
        def _():
            j = jnp.maximum(STEPS - 3 - 2 * p, 1)
            orbit_copy(j).wait_recv()
            force(j, first_ref)
            orbit_copy(j - 1).wait_recv()
            force(j - 1, second_ref)

        @pl.when(p == 0)
        def _():
            for side in range(2):
                lon_copy(pairs, side).wait_recv()

                @pl.when(comes[side])
                def _():
                    lat_copy(pairs, side).wait_recv()

        for side in range(2):
            @pl.when(comes[side])
            def _():
                lat_copy(p, side).wait_recv()
                diag_copy(p, side, 0).wait_recv()
                diag_copy(p, side, 1).wait_recv()

        for side in range(2):
            lon_copy(p, side).wait_recv()
            edge = (0, last)[side]
            halo_ref[0, :, edge, :] = lon_in[side, p, 0]

            far = (last, 0)[side]
            corner = [upright(diag_in[i, side, p, 0, far:far + 1, :]) for i in range(2)]
            beside = (lon_in[side, p, 1] + lon_out[1 - side, p, 0]
                      + jnp.where(wide_lane == 0, corner[0], 0.0)
                      + jnp.where(wide_lane == CLAT - 1, corner[1], 0.0))
            up = lon_in[side, pairs, 0, 0:levels - 1] * (beside[1:] - beside[:-1])
            mixed = (beside + jnp.concatenate([up, blank], axis=0)
                     - jnp.concatenate([blank, up], axis=0))
            halo_ref[1, :, edge, :] = lon_in[side, pairs, 1] * mixed

        rows, later = [], []
        for side in range(2):
            rows.append(lat_in[side, p, 0])
            beside = (lat_in[side, p, 1] + shed[1 - side]
                      + jnp.where(flat_sub == 0, pltpu.roll(diag_in[side, 0, p, 1], 1, 0), 0.0)
                      + jnp.where(flat_sub == last, pltpu.roll(diag_in[side, 1, p, 1], last, 0), 0.0))
            up = lat_in[side, pairs, 0] * (pltpu.roll(beside, CLAT - 1, 1) - beside)
            mixed = beside + up - pltpu.roll(up, 1, 1)
            later.append(lat_in[side, pairs, 1] * mixed)

        rows, later = weave(rows), weave(later)
        for a in tiles:
            here = slice(a, a + 8)
            more = halo_ref[0, here] + near(rows, a)
            if a == 0:
                flux_ref[...] += more[0]
            forced_ref[here] += more
        mix(None)
        for a in tiles:
            here = slice(a, a + 8)
            result = stencil(a) + (halo_ref[1, here] + near(later, a))
            if a == 0:
                flux_ref[...] += result[0]
            adjoint_ref[here] = result
            forced_ref[here] = result + first_ref[here]
        return 0

    first_ref[...] = jnp.zeros_like(first_ref)
    lax.fori_loop(0, pairs, advance, 0)

    def finish(p, _):
        for side in range(2):
            lon_copy(p, side).wait_send()

            @pl.when(towards[side])
            def _():
                lat_copy(p, side).wait_send()

            @pl.when(towards[side] & (p < pairs))
            def _():
                diag_copy(p, side, 0).wait_send()
                diag_copy(p, side, 1).wait_send()
        return 0

    lax.fori_loop(0, pairs + 1, finish, 0)

    def done(t, _):
        orbit_copy(t).wait_send()
        return 0

    lax.fori_loop(0, STEPS, done, 0)

    def parted(d, _):
        slot_copy(d).wait_send()
        return 0

    lax.fori_loop(1, owners, parted, 0)


def per_device(kernel, residual, owner_block, column, time_step, horizontal, vertical):
    orbits, lons, lats = (lax.axis_size(name) for name in ("orbit", "lon", "lat"))
    owners = lons * lats
    klevels, count = kernel.shape
    levels = horizontal.shape[1]
    slot_rows = 4 * count // owners // CLAT
    heights = -(-(count // CLAT + slot_rows + 1) // 8) * 8
    chunks = count // CHUNK
    block, flat = (levels, CLON, CLAT), (CLON, CLAT)
    turns = STEPS // 2 + 1
    slots = (owners, klevels + 1, slot_rows, CLAT)
    bins = (STEPS, klevels, CLON, CLAT)
    width = slot_rows * CLAT
    dma, row = pltpu.SemaphoreType.DMA, pltpu.VMEM((1, count), jnp.int32)
    inputs = (kernel, residual.reshape(1, count), owner_block.reshape(1, count),
              column.reshape(1, count), time_step.reshape(1, count), horizontal, vertical)
    vmem = pl.BlockSpec(memory_space=pltpu.VMEM)
    return pl.pallas_call(
        functools.partial(whole_kernel, orbits, lons, lats, level_weights(levels, klevels)),
        out_shape=(jax.ShapeDtypeStruct(block, F32), jax.ShapeDtypeStruct(flat, F32)),
        in_specs=[pl.BlockSpec(memory_space=pltpu.HBM)] * 7,
        out_specs=(vmem, vmem),
        scratch_shapes=[
            pltpu.VMEM(kernel.shape, F32), pltpu.VMEM((1, count), F32), row, row, row,
            pltpu.VMEM(horizontal.shape, F32), pltpu.VMEM(vertical.shape, F32),
            pltpu.VMEM((chunks * owners, CHUNK), BF16),
            pltpu.VMEM((2 * ROWS, count), BF16),
            row,
            pltpu.VMEM((2 * ROWS * chunks, min(count, 4 * CHUNK)), BF16),
            pltpu.VMEM((ROWS, heights, CLAT), F32),
            pltpu.VMEM(slots, F32), pltpu.VMEM(slots, F32),
            pltpu.VMEM((2 * STEPS * ROWS, CELLS), F32),
            pltpu.VMEM((2 * STEPS * ROWS, width), BF16),
            pltpu.VMEM((CELLS, width), BF16),
            pltpu.VMEM(bins, F32), pltpu.VMEM(bins, F32),
            pltpu.VMEM(block, F32), pltpu.VMEM(block, F32), pltpu.VMEM(block, F32),
            pltpu.VMEM((4,) + block, F32),
            pltpu.VMEM(block, F32), pltpu.VMEM(block, F32), pltpu.VMEM((2,) + block, F32),
            pltpu.VMEM((2, 2) + flat, F32),
            pltpu.VMEM((2, turns, 2, levels, CLAT), F32),
            pltpu.VMEM((2, turns, 2, levels, CLAT), F32),
            pltpu.VMEM((2, turns, 2) + flat, F32),
            pltpu.VMEM((2, turns, 2) + flat, F32),
            pltpu.VMEM((2, turns, 2) + flat, F32),
            pltpu.VMEM((2, 2, turns, 2) + flat, F32),
            dma((7,)), dma((owners,)), dma((owners,)), dma((STEPS,)), dma((STEPS,)),
            dma((2, turns)), dma((2, turns)), dma((2, turns)), dma((2, turns)),
            dma((2, 2, turns)), dma((2, 2, turns)),
        ],
        compiler_params=pltpu.CompilerParams(
            collective_id=0, has_side_effects=True, vmem_limit_bytes=VMEM_LIMIT),
    )(*(pltpu.with_memory_space_constraint(x, pltpu.HBM) for x in inputs))


def solution(mesh):
    placed = (
        P(None, ("orbit", "lon", "lat")),
        P(("orbit", "lon", "lat")),
        P(("orbit", "lon", "lat"), None),
        P(("orbit", "lon", "lat")),
        P(("orbit", "lon", "lat")),
        P(None, None, "lon", "lat"),
        P(None, "lon", "lat"),
    )
    return jax.shard_map(
        per_device,
        mesh=mesh,
        in_specs=placed,
        out_specs=(P(None, "lon", "lat"), P("lon", "lat")),
        check_vma=False,
    )
```

time: 86.8 us -> 75 us (0.86)
  Pallas kernels: 84.5 us -> 72.8 us
    pallas_call x3 -> x1, Pallas kernels: 84.5 us -> 72.8 us  [per_device(): pl.pallas_call(functools.partial(whole_kernel, orbits, lons, lats, level_...]
where the time goes in v4:
time: 75 us; the launch traced here: 74.7 us
  Pallas kernels  72.8 us (97%)
  local copies, waits for them, and re-layouts  1.31 us (2%)
    pallas_call x1, Pallas kernels, per_device(): pl.pallas_call(functools.partial(whole_kernel, orbits, lons, lats, level_...  72.8 us

profile of v4, /device:TPU:0, one launch (start us, length us, event | category | flops | bytes accessed | tf_op | source)
XLA Modules:
  0.0 74.7 jit_solution(14408855386335157524)
XLA Ops:
  0.6 72.8 %shard_map.86 = (f32[72,8,128]{2,1,0:T(8,128)S(1)}, f32[8,128]{1,0:T(8,128)S(1)}) custom-call(f32[20,4096]{1,0:T(8,128)} %kernel_hbm.1, f32[1,4096]{1,0:T(1,128)} %bitcast.4, s32[1,4096]{1,0:T(1,128)} %bitcast.5, s32[1,4096]{1,0:T(1,128)} %bitcast.6, s32[1,4096]{1,0:T(1,128)} %bitcast.7, f32[4,72,8,128]{3,2,1,0:T(8,128)} %horizontal_hbm.1, ...), custom_call_target="tpu_custom_call" | custom-call | tf_op jit(solution)/shard_map/pallas_call | solution.py:540
  73.4 0.7 copy.11
  74.1 0.6 copy.12

commit v5 on v4

--- a/solution.py
+++ b/solution.py
@@ -14,6 +14,7 @@
 CELLS = CLON * CLAT
 ROWS = 24
 CHUNK = 256
+RELAY_LONS = 4
 F32 = jnp.float32
 BF16 = jnp.bfloat16
 VMEM_LIMIT = 48 * 1024 * 1024
@@ -38,10 +39,10 @@
                  horizontal_hbm, vertical_hbm, adjoint_ref, flux_ref,
                  kernel_ref, residual_ref, owner_ref, column_ref, time_ref, horizontal_ref, vertical_ref,
                  own_ref, data_ref, place_ref, left_ref, sorted_ref,
-                 slots_ref, got_ref, total_ref, taken_ref, chosen_ref,
+                 slots_ref, got_ref, raw_ref, shared_ref, total_ref, taken_ref, chosen_ref,
                  bins_ref, other_ref, forced_ref, mixed_ref, diagonal_ref, weight_ref,
                  first_ref, second_ref, halo_ref, pack_ref, lon_out, lon_in, lat_out, lat_in,
-                 diag_out, diag_in, load_sem, slot_send, slot_recv, orbit_send, orbit_recv,
+                 diag_out, diag_in, load_sem, slot_send, slot_recv, raw_send, raw_recv, shared_send, orbit_send, orbit_recv,
                  lon_send, lon_recv, lat_send, lat_recv, diag_send, diag_recv):
     klevels, count = kernel_hbm.shape
     owners, _, slot_rows, _ = slots_ref.shape
@@ -79,6 +80,27 @@
             src_ref=slots_ref.at[to_lon * lats + to_lat], dst_ref=got_ref.at[d],
             send_sem=slot_send.at[d], recv_sem=slot_recv.at[d],
             device_id={"lon": to_lon, "lat": to_lat}, device_id_type=mesh_id)
+
+    relayed = lons == RELAY_LONS
+    central = (lon == 1) | (lon == 2) if relayed else None
+    planes = klevels + 2
+    via = jnp.where(lon == 1, 3, jnp.where(lon == 2, 1, 2))
+
+    def direct(d):
+        offset = d // lats
+        return jnp.logical_not(((lon == 1) & (offset >= 1) & (offset <= 2)) | ((lon == 2) & (offset >= 2)))
+
+    def raw_copy(source, turn):
+        return pltpu.make_async_remote_copy(
+            src_ref=source.at[0:planes, 0:filled], dst_ref=raw_ref.at[0:planes, 0:filled],
+            send_sem=raw_send.at[turn], recv_sem=raw_recv.at[0],
+            device_id={"lon": (3 - lon, (lon - 1) * 3)[turn]}, device_id_type=mesh_id)
+
+    def shared_copy(t):
+        return pltpu.make_async_remote_copy(
+            src_ref=shared_ref.at[t], dst_ref=got_ref.at[via * lats + t],
+            send_sem=shared_send.at[t], recv_sem=slot_recv.at[via * lats + t],
+            device_id={"lat": lax.rem(lat + t, lats)}, device_id_type=mesh_id)
 
     barrier = pltpu.get_barrier_semaphore()
     pl.semaphore_signal(barrier, inc=1, device_id={"orbit": partner}, device_id_type=mesh_id)
@@ -184,21 +206,39 @@
     slot_lane = lax.broadcasted_iota(jnp.int32, shape, 2)
     slot = (lax.broadcasted_iota(jnp.int32, (1, slot_rows, CLAT), 1) * CLAT
             + lax.broadcasted_iota(jnp.int32, (1, slot_rows, CLAT), 2))
-    first = [jnp.clip(jnp.max(starts[o:o + 1]).astype(jnp.int32), 0, count)
-             for o in range(owners)] + [count]
+    def scalar(row):
+        return jnp.clip(jnp.max(row).astype(jnp.int32), 0, count)
+
+    def hand_out(source, begins, ends_at):
+        row, shift = begins // CLAT, lax.rem(begins, CLAT)
+        back = lax.rem(CLAT - shift, CLAT)
+        one = pltpu.roll(source[0:klevels + 1, pl.ds(row, slot_rows), :], back, 2)
+        two = pltpu.roll(source[0:klevels + 1, pl.ds(row + 1, slot_rows), :], back, 2)
+        run = jnp.where(slot_lane < CLAT - shift, one, two)
+        return run[0:klevels], jnp.where(slot < ends_at - begins, run[klevels:], -1.0)
+
+    if relayed:
+        sorted_ref[klevels + 1, 0:owners, :] = starts
+        sorted_ref[klevels + 1, owners:owners + 8, :] = jnp.full((8, CLAT), float(count), F32)
+        raw_ref[:, filled:, :] = jnp.zeros((ROWS, heights - filled, CLAT), F32)
+
+        @pl.when(central)
+        def _():
+            raw_copy(sorted_ref, 0).start()
+
+    first = [scalar(starts[o:o + 1]) for o in range(owners)] + [count]
     for o in range(owners):
-        row, shift = first[o] // CLAT, lax.rem(first[o], CLAT)
-        back = lax.rem(CLAT - shift, CLAT)
-        one = pltpu.roll(sorted_ref[0:klevels + 1, pl.ds(row, slot_rows), :], back, 2)
-        two = pltpu.roll(sorted_ref[0:klevels + 1, pl.ds(row + 1, slot_rows), :], back, 2)
-        run = jnp.where(slot_lane < CLAT - shift, one, two)
-        slots_ref[o, 0:klevels] = run[0:klevels]
-        slots_ref[o, klevels:] = jnp.where(slot < first[o + 1] - first[o], run[klevels:], -1.0)
-
+        slots_ref[o, 0:klevels], slots_ref[o, klevels:] = hand_out(sorted_ref, first[o], first[o + 1])
 
     even_lon = lax.rem(lon, 2) == 0
 
     def send_turn(i):
+        if relayed:
+            early = i <= 2 * (lats - 1)
+            m = jnp.where(early, i // 2, i - lats)
+            ring = m // lats
+            offset = jnp.where(ring == 2, 2, jnp.where((ring == 0) == even_lon, 1, 3))
+            return jnp.where(early & (lax.rem(i, 2) == 0), i // 2, offset * lats + lax.rem(m, lats))
         m = jnp.where(lax.rem(i, 2) == 1, i // 2, owners // 2 + i // 2 - 1)
         ring = m // lats
         right = (lax.rem(ring, 2) == 1) == even_lon
@@ -207,14 +247,42 @@
 
     def turn(i):
         ring = i // lats
-        offset = jnp.where(even_lon, lax.rem(lons - ring, lons), ring)
+        if relayed:
+            offset = jnp.where(ring == 0, 0, jnp.where(ring == 3, 2, jnp.where(
+                (ring == 1) == even_lon, 3, 1)))
+        else:
+            offset = jnp.where(even_lon, lax.rem(lons - ring, lons), ring)
         return offset * lats + lax.rem(i, lats)
 
     def begin(i, _):
-        slot_copy(send_turn(i)).start()
+        d = send_turn(i)
+        if relayed:
+            @pl.when(direct(d))
+            def _():
+                slot_copy(d).start()
+        else:
+            slot_copy(d).start()
         return 0
 
     lax.fori_loop(1, owners, begin, 0)
+
+    def share():
+        raw_copy(sorted_ref, 0).wait_recv()
+
+        @pl.when(central)
+        def _():
+            raw_copy(raw_ref, 1).start()
+
+        for t in range(lats):
+            name = lon * lats + lax.rem(lat + t, lats)
+            values, segment = hand_out(raw_ref, scalar(raw_ref[klevels + 1, pl.ds(name, 1), :]),
+                                       scalar(raw_ref[klevels + 1, pl.ds(name + 1, 1), :]))
+            if t == 0:
+                got_ref[via * lats, 0:klevels], got_ref[via * lats, klevels:] = values, segment
+            else:
+                shared_ref[t, 0:klevels], shared_ref[t, klevels:] = values, segment
+                shared_copy(t).start()
+
     total_ref[...] = jnp.zeros_like(total_ref)
     got_ref[0] = slots_ref[lon * lats + lat]
 
@@ -276,7 +344,12 @@
     def gain(i, _):
         d = turn(i)
 
-        @pl.when(i > 0)
+        if relayed:
+            @pl.when(i == jnp.where(central, lats, 2 * lats))
+            def _():
+                share()
+
+        @pl.when((i > 0) & (d != via * lats) if relayed else i > 0)
         def _():
             slot_copy(d).wait_recv()
 
@@ -514,10 +587,23 @@
     lax.fori_loop(0, STEPS, done, 0)
 
     def parted(d, _):
-        slot_copy(d).wait_send()
+        if relayed:
+            @pl.when(direct(d))
+            def _():
+                slot_copy(d).wait_send()
+        else:
+            slot_copy(d).wait_send()
         return 0
 
     lax.fori_loop(1, owners, parted, 0)
+    if relayed:
+        for t in range(1, lats):
+            shared_copy(t).wait_send()
+
+        @pl.when(central)
+        def _():
+            raw_copy(sorted_ref, 0).wait_send()
+            raw_copy(raw_ref, 1).wait_send()
 
 
 def per_device(kernel, residual, owner_block, column, time_step, horizontal, vertical):
@@ -551,6 +637,7 @@
             pltpu.VMEM((2 * ROWS * chunks, min(count, 4 * CHUNK)), BF16),
             pltpu.VMEM((ROWS, heights, CLAT), F32),
             pltpu.VMEM(slots, F32), pltpu.VMEM(slots, F32),
+            pltpu.VMEM((ROWS, heights, CLAT), F32), pltpu.VMEM((lats,) + slots[1:], F32),
             pltpu.VMEM((2 * STEPS * ROWS, CELLS), F32),
             pltpu.VMEM((2 * STEPS * ROWS, width), BF16),
             pltpu.VMEM((CELLS, width), BF16),
@@ -565,7 +652,7 @@
             pltpu.VMEM((2, turns, 2) + flat, F32),
             pltpu.VMEM((2, turns, 2) + flat, F32),
             pltpu.VMEM((2, 2, turns, 2) + flat, F32),
-            dma((7,)), dma((owners,)), dma((owners,)), dma((STEPS,)), dma((STEPS,)),
+            dma((7,)), dma((owners,)), dma((owners,)), dma((2,)), dma((1,)), dma((lats,)), dma((STEPS,)), dma((STEPS,)),
             dma((2, turns)), dma((2, turns)), dma((2, turns)), dma((2, turns)),
             dma((2, 2, turns)), dma((2, 2, turns)),
         ],

time: 75 us -> 84.1 us (1.12)
  Pallas kernels: 72.8 us -> 81.9 us
    pallas_call x1, Pallas kernels: 72.8 us -> 81.9 us  [per_device(): pl.pallas_call(functools.partial(whole_kernel, orbits, lons, lats, level_...]
where the time goes in v5:
time: 84.1 us; the launch traced here: 83.8 us
  Pallas kernels  81.9 us (97%)
  local copies, waits for them, and re-layouts  1.31 us (2%)
    pallas_call x1, Pallas kernels, per_device(): pl.pallas_call(functools.partial(whole_kernel, orbits, lons, lats, level_...  81.9 us

profile of v5, /device:TPU:0, one launch (start us, length us, event | category | flops | bytes accessed | tf_op | source)
XLA Modules:
  0.0 83.8 jit_solution(9856446422328466801)
XLA Ops:
  0.6 81.9 %shard_map.86 = (f32[72,8,128]{2,1,0:T(8,128)S(1)}, f32[8,128]{1,0:T(8,128)S(1)}) custom-call(f32[20,4096]{1,0:T(8,128)} %kernel_hbm.1, f32[1,4096]{1,0:T(1,128)} %bitcast.4, s32[1,4096]{1,0:T(1,128)} %bitcast.5, s32[1,4096]{1,0:T(1,128)} %bitcast.6, s32[1,4096]{1,0:T(1,128)} %bitcast.7, f32[4,72,8,128]{3,2,1,0:T(8,128)} %horizontal_hbm.1, ...), custom_call_target="tpu_custom_call" | custom-call | tf_op jit(solution)/shard_map/pallas_call | solution.py:626
  82.5 0.7 copy.11
  83.2 0.6 copy.12

commit v6 on v4

--- a/solution.py
+++ b/solution.py
@@ -40,7 +40,7 @@
                  own_ref, data_ref, place_ref, left_ref, sorted_ref,
                  slots_ref, got_ref, total_ref, taken_ref, chosen_ref,
                  bins_ref, other_ref, forced_ref, mixed_ref, diagonal_ref, weight_ref,
-                 first_ref, second_ref, halo_ref, pack_ref, lon_out, lon_in, lat_out, lat_in,
+                 first_ref, second_ref, halo_ref, pack_ref, corner_ref, lon_out, lon_in, lat_out, lat_in,
                  diag_out, diag_in, load_sem, slot_send, slot_recv, orbit_send, orbit_recv,
                  lon_send, lon_recv, lat_send, lat_recv, diag_send, diag_recv):
     klevels, count = kernel_hbm.shape
@@ -111,7 +111,7 @@
 
     def diag_copy(p, side, turn):
         return pltpu.make_async_remote_copy(
-            src_ref=diag_out.at[side, p], dst_ref=diag_in.at[side, turn, p],
+            src_ref=diag_out.at[side, turn, p], dst_ref=diag_in.at[side, turn, p],
             send_sem=diag_send.at[side, turn, p], recv_sem=diag_recv.at[side, turn, p],
             device_id={"lon": (east, west)[turn], "lat": (lat + 1, lat - 1)[side]},
             device_id_type=mesh_id)
@@ -273,7 +273,7 @@
         def _():
             lat_copy(pairs, side).start()
 
-    def gain(i, _):
+    def take(i):
         d = turn(i)
 
         @pl.when(i > 0)
@@ -297,13 +297,21 @@
             key = jnp.broadcast_to(key, (CLAT, width)).astype(BF16)
             chosen_ref[i * CLAT:(i + 1) * CLAT] = jnp.where(
                 key == cell, jnp.ones((), BF16), jnp.zeros((), BF16))
+
+    def gain(i, _):
+        take(i)
         total_ref[...] += lax.dot_general(
             taken_ref[...], chosen_ref[...], NT, preferred_element_type=F32)
         return 0
 
-    lax.fori_loop(0, owners, gain, 0)
+    lax.fori_loop(0, owners - 1, gain, 0)
+    take(owners - 1)
     for j in range(STEPS - 1, -1, -1):
         top = j * 2 * ROWS
+        if j >= STEPS - 2 or j == STEPS - 3:
+            low = top if j >= STEPS - 2 else 0
+            total_ref[low:top + 2 * ROWS] += lax.dot_general(
+                taken_ref[low:top + 2 * ROWS], chosen_ref[...], NT, preferred_element_type=F32)
         cells = total_ref[top:top + klevels] + total_ref[top + ROWS:top + ROWS + klevels]
         for i in range(CLON):
             bins_ref[j, :, i, :] = cells[:, i * CLAT:(i + 1) * CLAT]
@@ -363,9 +371,16 @@
     wide_level = lax.broadcasted_iota(jnp.int32, wide, 0)
     blank = jnp.zeros((1, CLAT), F32)
 
-    def upright(row):
-        return jnp.sum(jnp.where(wide_lane == wide_level, jnp.broadcast_to(row, wide), 0.0),
-                       axis=1, keepdims=True)
+    def level_row(column):
+        return jnp.sum(jnp.where(wide_lane == wide_level, jnp.broadcast_to(column, wide), 0.0),
+                       axis=0, keepdims=True)
+
+    def corners(first, second):
+        return jnp.where(flat_sub == 0, first, jnp.where(flat_sub == last, second, 0.0))
+
+    def mix_rows(rows, weight):
+        up = weight * (pltpu.roll(rows, CLAT - 1, 1) - rows)
+        return rows + up - pltpu.roll(up, 1, 1)
 
     def advance(p, _):
         packed = gather()
@@ -376,8 +391,11 @@
             out = pack_ref[side, 0] * packed[side]
             shed.append(out)
             lat_out[side, p, 0] = out
-            diag_out[side, p, 0] = out
-            diag_out[side, p, 1] = pack_ref[side, 1] * packed[side]
+            mingled = pack_ref[side, 1] * packed[side]
+            for turn_to in range(2):
+                far = (last, 0)[turn_to]
+                diag_out[side, turn_to, p, 0:1] = out[far:far + 1]
+                diag_out[side, turn_to, p, 1:2] = mingled[far:far + 1]
 
             @pl.when(towards[side])
             def _():
@@ -438,40 +456,29 @@
                 @pl.when(comes[side])
                 def _():
                     lat_copy(pairs, side).wait_recv()
+            for side in range(2):
+                end = (0, CLAT - 1)[side]
+                for which in range(2):
+                    corner_ref[side, which] = corners(*(
+                        level_row(lon_in[turn, pairs, which, :, end:end + 1]) for turn in range(2)))
 
         for side in range(2):
             @pl.when(comes[side])
             def _():
                 lat_copy(p, side).wait_recv()
-                diag_copy(p, side, 0).wait_recv()
-                diag_copy(p, side, 1).wait_recv()
 
         for side in range(2):
             lon_copy(p, side).wait_recv()
             edge = (0, last)[side]
             halo_ref[0, :, edge, :] = lon_in[side, p, 0]
 
-            far = (last, 0)[side]
-            corner = [upright(diag_in[i, side, p, 0, far:far + 1, :]) for i in range(2)]
-            beside = (lon_in[side, p, 1] + lon_out[1 - side, p, 0]
-                      + jnp.where(wide_lane == 0, corner[0], 0.0)
-                      + jnp.where(wide_lane == CLAT - 1, corner[1], 0.0))
+            beside = lon_in[side, p, 1] + lon_out[1 - side, p, 0]
             up = lon_in[side, pairs, 0, 0:levels - 1] * (beside[1:] - beside[:-1])
             mixed = (beside + jnp.concatenate([up, blank], axis=0)
                      - jnp.concatenate([blank, up], axis=0))
             halo_ref[1, :, edge, :] = lon_in[side, pairs, 1] * mixed
 
-        rows, later = [], []
-        for side in range(2):
-            rows.append(lat_in[side, p, 0])
-            beside = (lat_in[side, p, 1] + shed[1 - side]
-                      + jnp.where(flat_sub == 0, pltpu.roll(diag_in[side, 0, p, 1], 1, 0), 0.0)
-                      + jnp.where(flat_sub == last, pltpu.roll(diag_in[side, 1, p, 1], last, 0), 0.0))
-            up = lat_in[side, pairs, 0] * (pltpu.roll(beside, CLAT - 1, 1) - beside)
-            mixed = beside + up - pltpu.roll(up, 1, 1)
-            later.append(lat_in[side, pairs, 1] * mixed)
-
-        rows, later = weave(rows), weave(later)
+        rows = weave([lat_in[side, p, 0] for side in range(2)])
         for a in tiles:
             here = slice(a, a + 8)
             more = halo_ref[0, here] + near(rows, a)
@@ -479,6 +486,20 @@
                 flux_ref[...] += more[0]
             forced_ref[here] += more
         mix(None)
+        for side in range(2):
+            @pl.when(comes[side])
+            def _():
+                diag_copy(p, side, 0).wait_recv()
+                diag_copy(p, side, 1).wait_recv()
+
+        later = []
+        for side in range(2):
+            turned = [corners(diag_in[side, 0, p, which:which + 1],
+                              diag_in[side, 1, p, which:which + 1]) for which in range(2)]
+            beside = lat_in[side, p, 1] + shed[1 - side] + turned[1]
+            later.append(lat_in[side, pairs, 1] * mix_rows(beside, lat_in[side, pairs, 0])
+                         + corner_ref[side, 1] * mix_rows(turned[0], corner_ref[side, 0]))
+        later = weave(later)
         for a in tiles:
             here = slice(a, a + 8)
             result = stencil(a) + (halo_ref[1, here] + near(later, a))
@@ -559,12 +580,13 @@
             pltpu.VMEM((4,) + block, F32),
             pltpu.VMEM(block, F32), pltpu.VMEM(block, F32), pltpu.VMEM((2,) + block, F32),
             pltpu.VMEM((2, 2) + flat, F32),
+            pltpu.VMEM((2, 2) + flat, F32),
             pltpu.VMEM((2, turns, 2, levels, CLAT), F32),
             pltpu.VMEM((2, turns, 2, levels, CLAT), F32),
             pltpu.VMEM((2, turns, 2) + flat, F32),
             pltpu.VMEM((2, turns, 2) + flat, F32),
-            pltpu.VMEM((2, turns, 2) + flat, F32),
-            pltpu.VMEM((2, 2, turns, 2) + flat, F32),
+            pltpu.VMEM((2, 2, turns, 2, CLAT), F32),
+            pltpu.VMEM((2, 2, turns, 2, CLAT), F32),
             dma((7,)), dma((owners,)), dma((owners,)), dma((STEPS,)), dma((STEPS,)),
             dma((2, turns)), dma((2, turns)), dma((2, turns)), dma((2, turns)),
             dma((2, 2, turns)), dma((2, 2, turns)),

time: 75 us -> 73.6 us (0.981)
  Pallas kernels: 72.8 us -> 71.4 us
    pallas_call x1, Pallas kernels: 72.8 us -> 71.4 us  [per_device(): pl.pallas_call(functools.partial(whole_kernel, orbits, lons, lats, level_...]
where the time goes in v6:
time: 73.6 us; the launch traced here: 73.4 us
  Pallas kernels  71.4 us (97%)
  local copies, waits for them, and re-layouts  1.31 us (2%)
    pallas_call x1, Pallas kernels, per_device(): pl.pallas_call(functools.partial(whole_kernel, orbits, lons, lats, level_...  71.4 us

profile of v6, /device:TPU:0, one launch (start us, length us, event | category | flops | bytes accessed | tf_op | source)
XLA Modules:
  0.0 73.4 jit_solution(11520042208580952780)
XLA Ops:
  0.6 71.4 %shard_map.86 = (f32[72,8,128]{2,1,0:T(8,128)S(1)}, f32[8,128]{1,0:T(8,128)S(1)}) custom-call(f32[20,4096]{1,0:T(8,128)} %kernel_hbm.1, f32[1,4096]{1,0:T(1,128)} %bitcast.4, s32[1,4096]{1,0:T(1,128)} %bitcast.5, s32[1,4096]{1,0:T(1,128)} %bitcast.6, s32[1,4096]{1,0:T(1,128)} %bitcast.7, f32[4,72,8,128]{3,2,1,0:T(8,128)} %horizontal_hbm.1, ...), custom_call_target="tpu_custom_call" | custom-call | tf_op jit(solution)/shard_map/pallas_call | solution.py:561
  72.1 0.7 copy.11
  72.8 0.6 copy.12

commit v7 on v6

--- a/solution.py
+++ b/solution.py
@@ -97,10 +97,10 @@
             send_sem=orbit_send.at[j], recv_sem=orbit_recv.at[j],
             device_id={"orbit": partner}, device_id_type=mesh_id)
 
-    def lon_copy(p, side):
+    def lon_copy(p, side, which):
         return pltpu.make_async_remote_copy(
-            src_ref=lon_out.at[side, p], dst_ref=lon_in.at[side, p],
-            send_sem=lon_send.at[side, p], recv_sem=lon_recv.at[side, p],
+            src_ref=lon_out.at[side, p, which], dst_ref=lon_in.at[side, p, which],
+            send_sem=lon_send.at[side, p, which], recv_sem=lon_recv.at[side, p, which],
             device_id={"lon": (east, west)[side]}, device_id_type=mesh_id)
 
     def lat_copy(p, side):
@@ -146,7 +146,8 @@
         lon_out[side, pairs, 0, 0:levels - 1] = vertical_ref[:, edge, :]
         lon_out[side, pairs, 0, levels - 1:] = jnp.zeros((1, CLAT), F32)
         lon_out[side, pairs, 1] = horizontal_ref[side, :, edge, :]
-        lon_copy(pairs, side).start()
+        lon_copy(pairs, side, 0).start()
+        lon_copy(pairs, side, 1).start()
 
     for load in loads[1:5]:
         load.wait()
@@ -402,26 +403,31 @@
                 diag_copy(p, side, 0).start()
                 diag_copy(p, side, 1).start()
 
+        def send_lon(which):
+            @pl.when(lon == 0)
+            def _():
+                lon_copy(p, 1, which).start()
+                lon_copy(p, 0, which).start()
+
+            @pl.when(lon > 0)
+            def _():
+                lon_copy(p, 0, which).start()
+                lon_copy(p, 1, which).start()
+
+        for side in range(2):
+            edge = (last, 0)[side]
+            lon_out[side, p, 0] = horizontal_ref[side, :, edge, :] * mixed_ref[:, edge, :]
+        send_lon(0)
         for side in range(2):
             edge, inner = ((last, last - 1), (0, 1))[side]
             mixed = mixed_ref[:, edge, :]
-            lon_out[side, p, 0] = horizontal_ref[side, :, edge, :] * mixed
             lon_out[side, p, 1] = (
                 diagonal_ref[:, edge, :] * mixed
                 + weight_ref[side, :, edge, :] * mixed_ref[:, inner, :]
                 + weight_ref[2, :, edge, :] * pltpu.roll(mixed, 1, 1)
                 + weight_ref[3, :, edge, :] * pltpu.roll(mixed, CLAT - 1, 1)
                 + second_ref[:, edge, :])
-
-        @pl.when(lon == 0)
-        def _():
-            lon_copy(p, 1).start()
-            lon_copy(p, 0).start()
-
-        @pl.when(lon > 0)
-        def _():
-            lon_copy(p, 0).start()
-            lon_copy(p, 1).start()
+        send_lon(1)
 
         partial = gather()
         for a in tiles:
@@ -451,7 +457,8 @@
         @pl.when(p == 0)
         def _():
             for side in range(2):
-                lon_copy(pairs, side).wait_recv()
+                lon_copy(pairs, side, 0).wait_recv()
+                lon_copy(pairs, side, 1).wait_recv()
 
                 @pl.when(comes[side])
                 def _():
@@ -468,15 +475,8 @@
                 lat_copy(p, side).wait_recv()
 
         for side in range(2):
-            lon_copy(p, side).wait_recv()
-            edge = (0, last)[side]
-            halo_ref[0, :, edge, :] = lon_in[side, p, 0]
-
-            beside = lon_in[side, p, 1] + lon_out[1 - side, p, 0]
-            up = lon_in[side, pairs, 0, 0:levels - 1] * (beside[1:] - beside[:-1])
-            mixed = (beside + jnp.concatenate([up, blank], axis=0)
-                     - jnp.concatenate([blank, up], axis=0))
-            halo_ref[1, :, edge, :] = lon_in[side, pairs, 1] * mixed
+            lon_copy(p, side, 0).wait_recv()
+            halo_ref[0, :, (0, last)[side], :] = lon_in[side, p, 0]
 
         rows = weave([lat_in[side, p, 0] for side in range(2)])
         for a in tiles:
@@ -486,6 +486,14 @@
                 flux_ref[...] += more[0]
             forced_ref[here] += more
         mix(None)
+        for side in range(2):
+            lon_copy(p, side, 1).wait_recv()
+            beside = lon_in[side, p, 1] + lon_out[1 - side, p, 0]
+            up = lon_in[side, pairs, 0, 0:levels - 1] * (beside[1:] - beside[:-1])
+            mixed = (beside + jnp.concatenate([up, blank], axis=0)
+                     - jnp.concatenate([blank, up], axis=0))
+            halo_ref[1, :, (0, last)[side], :] = lon_in[side, pairs, 1] * mixed
+
         for side in range(2):
             @pl.when(comes[side])
             def _():
@@ -514,7 +522,8 @@
 
     def finish(p, _):
         for side in range(2):
-            lon_copy(p, side).wait_send()
+            lon_copy(p, side, 0).wait_send()
+            lon_copy(p, side, 1).wait_send()
 
             @pl.when(towards[side])
             def _():
@@ -588,7 +597,7 @@
             pltpu.VMEM((2, 2, turns, 2, CLAT), F32),
             pltpu.VMEM((2, 2, turns, 2, CLAT), F32),
             dma((7,)), dma((owners,)), dma((owners,)), dma((STEPS,)), dma((STEPS,)),
-            dma((2, turns)), dma((2, turns)), dma((2, turns)), dma((2, turns)),
+            dma((2, turns, 2)), dma((2, turns, 2)), dma((2, turns)), dma((2, turns)),
             dma((2, 2, turns)), dma((2, 2, turns)),
         ],
         compiler_params=pltpu.CompilerParams(

time: 73.6 us -> 73.1 us (level)
  no operation moved by 1% of the time
where the time goes in v7:
time: 73.1 us; the launch traced here: 72.9 us
  Pallas kernels  70.9 us (97%)
  local copies, waits for them, and re-layouts  1.31 us (2%)
    pallas_call x1, Pallas kernels, per_device(): pl.pallas_call(functools.partial(whole_kernel, orbits, lons, lats, level_...  70.9 us

profile of v7, /device:TPU:0, one launch (start us, length us, event | category | flops | bytes accessed | tf_op | source)
XLA Modules:
  0.0 72.9 jit_solution(9512667927188503027)
XLA Ops:
  0.6 70.9 %shard_map.86 = (f32[72,8,128]{2,1,0:T(8,128)S(1)}, f32[8,128]{1,0:T(8,128)S(1)}) custom-call(f32[20,4096]{1,0:T(8,128)} %kernel_hbm.1, f32[1,4096]{1,0:T(1,128)} %bitcast.4, s32[1,4096]{1,0:T(1,128)} %bitcast.5, s32[1,4096]{1,0:T(1,128)} %bitcast.6, s32[1,4096]{1,0:T(1,128)} %bitcast.7, f32[4,72,8,128]{3,2,1,0:T(8,128)} %horizontal_hbm.1, ...), custom_call_target="tpu_custom_call" | custom-call | tf_op jit(solution)/shard_map/pallas_call | solution.py:570
  71.6 0.7 copy.11
  72.3 0.6 copy.12

commit v8 on v7

--- a/solution.py
+++ b/solution.py
@@ -37,7 +37,7 @@
 def whole_kernel(orbits, lons, lats, weights, kernel_hbm, residual_hbm, owner_hbm, column_hbm, time_hbm,
                  horizontal_hbm, vertical_hbm, adjoint_ref, flux_ref,
                  kernel_ref, residual_ref, owner_ref, column_ref, time_ref, horizontal_ref, vertical_ref,
-                 own_ref, data_ref, place_ref, left_ref, sorted_ref,
+                 own_ref, data_ref, place_ref, left_ref, sorted_ref, bound_ref,
                  slots_ref, got_ref, total_ref, taken_ref, chosen_ref,
                  bins_ref, other_ref, forced_ref, mixed_ref, diagonal_ref, weight_ref,
                  first_ref, second_ref, halo_ref, pack_ref, corner_ref, lon_out, lon_in, lat_out, lat_in,
@@ -187,15 +187,18 @@
             + lax.broadcasted_iota(jnp.int32, (1, slot_rows, CLAT), 2))
     first = [jnp.clip(jnp.max(starts[o:o + 1]).astype(jnp.int32), 0, count)
              for o in range(owners)] + [count]
-    for o in range(owners):
-        row, shift = first[o] // CLAT, lax.rem(first[o], CLAT)
+    for o in range(owners + 1):
+        bound_ref[o] = first[o]
+
+    def hand_out(o, into):
+        begins = bound_ref[o]
+        row, shift = begins // CLAT, lax.rem(begins, CLAT)
         back = lax.rem(CLAT - shift, CLAT)
         one = pltpu.roll(sorted_ref[0:klevels + 1, pl.ds(row, slot_rows), :], back, 2)
         two = pltpu.roll(sorted_ref[0:klevels + 1, pl.ds(row + 1, slot_rows), :], back, 2)
         run = jnp.where(slot_lane < CLAT - shift, one, two)
-        slots_ref[o, 0:klevels] = run[0:klevels]
-        slots_ref[o, klevels:] = jnp.where(slot < first[o + 1] - first[o], run[klevels:], -1.0)
-
+        into[0:klevels] = run[0:klevels]
+        into[klevels:] = jnp.where(slot < bound_ref[o + 1] - begins, run[klevels:], -1.0)
 
     even_lon = lax.rem(lon, 2) == 0
 
@@ -212,12 +215,16 @@
         return offset * lats + lax.rem(i, lats)
 
     def begin(i, _):
-        slot_copy(send_turn(i)).start()
+        d = send_turn(i)
+        to_lon, to_lat = peer(d)
+        o = to_lon * lats + to_lat
+        hand_out(o, slots_ref.at[o])
+        slot_copy(d).start()
         return 0
 
     lax.fori_loop(1, owners, begin, 0)
     total_ref[...] = jnp.zeros_like(total_ref)
-    got_ref[0] = slots_ref[lon * lats + lat]
+    hand_out(lon * lats + lat, got_ref.at[0])
 
     for side in range(2):
         @pl.when(jnp.logical_not(comes[side]))
@@ -580,6 +587,7 @@
             row,
             pltpu.VMEM((2 * ROWS * chunks, min(count, 4 * CHUNK)), BF16),
             pltpu.VMEM((ROWS, heights, CLAT), F32),
+            pltpu.SMEM((owners + 1,), jnp.int32),
             pltpu.VMEM(slots, F32), pltpu.VMEM(slots, F32),
             pltpu.VMEM((2 * STEPS * ROWS, CELLS), F32),
             pltpu.VMEM((2 * STEPS * ROWS, width), BF16),

time: 73.1 us -> 72.8 us (level)
  no operation moved by 1% of the time
where the time goes in v8:
time: 72.8 us; the launch traced here: 72.6 us
  Pallas kernels  70.6 us (97%)
  local copies, waits for them, and re-layouts  1.31 us (2%)
    pallas_call x1, Pallas kernels, per_device(): pl.pallas_call(functools.partial(whole_kernel, orbits, lons, lats, level_...  70.6 us

profile of v8, /device:TPU:0, one launch (start us, length us, event | category | flops | bytes accessed | tf_op | source)
XLA Modules:
  0.0 72.6 jit_solution(5005088428243462263)
XLA Ops:
  0.6 70.6 %shard_map.86 = (f32[72,8,128]{2,1,0:T(8,128)S(1)}, f32[8,128]{1,0:T(8,128)S(1)}) custom-call(f32[20,4096]{1,0:T(8,128)} %kernel_hbm.1, f32[1,4096]{1,0:T(1,128)} %bitcast.4, s32[1,4096]{1,0:T(1,128)} %bitcast.5, s32[1,4096]{1,0:T(1,128)} %bitcast.6, s32[1,4096]{1,0:T(1,128)} %bitcast.7, f32[4,72,8,128]{3,2,1,0:T(8,128)} %horizontal_hbm.1, ...), custom_call_target="tpu_custom_call" | custom-call | tf_op jit(solution)/shard_map/pallas_call | solution.py:577
  71.3 0.7 copy.11
  72.0 0.6 copy.12
